TPU v7x, 256 devices: a whole 4x4x8 slice. The times are simulated.
256 devices in a mesh: dom: 32 (over y, z), feat: 8 (over x, core).
Axes of the slice: x: 4, y: 4, z: 8, core: 2. Of those that a mesh axis runs over, the one named last changes fastest.
Arguments:
- feats: bfloat16 [128, 262144], P('feat', 'dom'), may hold values from -6 to 6
- tile_vals: bfloat16 [10240, 128, 128], P('dom'), may hold values from -0.1875 to 0.1875
- tile_dst: int32 [10240], P('dom'), may hold values from 0 to 63
- tile_src: int32 [10240], P('dom'), may hold values from 0 to 111
- tile_count: int32 [32], P('dom'), may hold values from 80 to 320, as said below
- send_rows: int32 [32, 32, 64], P('dom'), may hold values from 0 to 8191
- hub_ids: int32 [4096], P('dom'), may hold values from 0 to 8191, as said below
- w_self: bfloat16 [128, 128], P('feat'), may hold values from -0.5 to 0.5
- w_neigh: bfloat16 [128, 128], P('feat'), may hold values from -0.5 to 0.5
- bias: float32 [128], P('feat'), may hold values from -3 to 3
- cotangent: bfloat16 [128, 262144], P('feat', 'dom'), may hold values from -6 to 6
Outputs:
- activated: bfloat16 [128, 262144], P('feat', 'dom')
- grad_feats: bfloat16 [128, 262144], P('feat', 'dom')
- grad_w_self: float32 [128, 128], P('feat')
- grad_w_neigh: float32 [128, 128], P('feat')
- grad_bias: float32 [128], P('feat')
Inputs may be any that keep to these rules, and one draw needn't show every extreme that they name: `tile_count`: the live tiles of a partition are its first ones; some partition has all 320 slots live. `hub_ids`: the 128 entries of one partition are distinct rows of that partition.
All inputs are finite; a program needn't handle non-finite values.
Results may differ from a plain program's by a relative error of at most 0.0075.
Values may be sent and summed in bfloat16 or wider, within the bound.
No kernel may reach another device: no remote copies, remote signals or barrier semaphores. Data moves between devices by JAX's collectives and lax.ppermute only.
A program may use at most 64 MiB of HBM per device.

v0:
```python
import math

import jax
import jax.numpy as jnp
from jax import lax
from jax.sharding import PartitionSpec as P

tile_edge = 128


def silu_slope(values):
    logistic = jax.nn.sigmoid(values)
    return logistic * (1.0 + values * (1.0 - logistic))


def as_blocks(matrix):
    return matrix.reshape(matrix.shape[0], matrix.shape[1] // tile_edge, tile_edge).transpose(
        1, 0, 2
    )


def from_blocks(blocks):
    return blocks.transpose(1, 0, 2).reshape(blocks.shape[1], blocks.shape[0] * tile_edge)


def tile_loop(tile_vals, tile_targets, tile_sources, live_count, step_fn, initial):
    group_size = math.gcd(tile_vals.shape[0], 128)
    group_total = (live_count + group_size - 1) // group_size

    def advance(group_index, totals):
        first_slot = group_index * group_size
        tile_block = lax.dynamic_slice_in_dim(tile_vals, first_slot, group_size, 0)
        targets = lax.dynamic_slice_in_dim(tile_targets, first_slot, group_size, 0)
        sources = lax.dynamic_slice_in_dim(tile_sources, first_slot, group_size, 0)
        is_live = first_slot + jnp.arange(group_size, dtype=jnp.int32) < live_count
        return step_fn(totals, tile_block, targets, sources, is_live)

    return lax.fori_loop(0, group_total, advance, initial)


def selector(indices, is_live, block_total):
    match = indices[:, None] == jnp.arange(block_total, dtype=jnp.int32)[None, :]
    return jnp.where(match & is_live[:, None], 1.0, 0.0).astype(jnp.float32)


def gather_step(extended_blocks):

    def step_fn(totals, tile_block, targets, sources, is_live):
        picked = extended_blocks[sources]
        products = jnp.einsum(
            "gfs,gds->gfd", picked, tile_block, preferred_element_type=jnp.float32
        )
        weights = selector(targets, is_live, totals.shape[0])
        return totals + jnp.einsum(
            "gb,gfd->bfd", weights, products, precision=lax.Precision.HIGHEST
        )

    return step_fn


def scatter_step(target_blocks):

    def step_fn(totals, tile_block, targets, sources, is_live):
        picked = target_blocks[targets]
        products = jnp.einsum(
            "gfd,gds->gfs", picked, tile_block, preferred_element_type=jnp.float32
        )
        weights = selector(sources, is_live, totals.shape[0])
        return totals + jnp.einsum(
            "gb,gfs->bfs", weights, products, precision=lax.Precision.HIGHEST
        )

    return step_fn


def local(
    feats,
    tile_vals,
    tile_dst,
    tile_src,
    tile_count,
    send_rows,
    hub_ids,
    w_self,
    w_neigh,
    bias,
    cotangent,
):
    width_here, node_rows = feats.shape
    domains = lax.axis_size("dom")
    send_list = send_rows[0].reshape(-1)
    outgoing = jnp.take(feats, send_list, axis=1)
    received = lax.all_to_all(outgoing, "dom", split_axis=1, concat_axis=1, tiled=True)
    hub_local = jnp.take(feats, hub_ids, axis=1)
    hub_table = lax.all_gather(hub_local, "dom", axis=1, tiled=True)
    extended = jnp.concatenate([feats, received, hub_table], axis=1)
    live_count = tile_count[0]
    empty_nodes = jnp.zeros((node_rows // tile_edge, width_here, tile_edge), jnp.float32)
    summed = tile_loop(
        tile_vals, tile_dst, tile_src, live_count, gather_step(as_blocks(extended)), empty_nodes
    )
    aggregate = from_blocks(summed).astype(jnp.bfloat16)
    full_feats, full_aggregate, self_full, neigh_full = (
        lax.all_gather(feats, "feat", axis=0, tiled=True),
        lax.all_gather(aggregate, "feat", axis=0, tiled=True),
        lax.all_gather(w_self, "feat", axis=0, tiled=True),
        lax.all_gather(w_neigh, "feat", axis=0, tiled=True),
    )
    first_column = lax.axis_index("feat") * width_here
    self_columns = lax.dynamic_slice_in_dim(self_full, first_column, width_here, 1)
    neigh_columns = lax.dynamic_slice_in_dim(neigh_full, first_column, width_here, 1)
    linear = jnp.einsum("io,in->on", self_columns, full_feats, preferred_element_type=jnp.float32)
    linear = linear + jnp.einsum(
        "io,in->on", neigh_columns, full_aggregate, preferred_element_type=jnp.float32
    )
    linear = linear + bias[:, None]
    activated = jax.nn.silu(linear).astype(jnp.bfloat16)
    grad_linear = (cotangent.astype(jnp.float32) * silu_slope(linear)).astype(jnp.bfloat16)
    grad_full = lax.all_gather(grad_linear, "feat", axis=0, tiled=True)
    grad_self = jnp.einsum("in,on->io", feats, grad_full, preferred_element_type=jnp.float32)
    grad_neigh = jnp.einsum("in,on->io", aggregate, grad_full, preferred_element_type=jnp.float32)
    grad_bias = jnp.sum(grad_linear.astype(jnp.float32), axis=1)
    grad_self, grad_neigh, grad_bias = lax.psum((grad_self, grad_neigh, grad_bias), "dom")
    scale = 1.0 / math.sqrt(node_rows * domains)
    grad_aggregate = jnp.einsum(
        "io,on->in", w_neigh, grad_full, preferred_element_type=jnp.float32
    ).astype(jnp.bfloat16)
    grad_feats = jnp.einsum("io,on->in", w_self, grad_full, preferred_element_type=jnp.float32)
    empty_extended = jnp.zeros((extended.shape[1] // tile_edge, width_here, tile_edge), jnp.float32)
    spread = tile_loop(
        tile_vals,
        tile_dst,
        tile_src,
        live_count,
        scatter_step(as_blocks(grad_aggregate)),
        empty_extended,
    )
    spread = from_blocks(spread)
    recv_total = received.shape[1]
    grad_feats = grad_feats + spread[:, :node_rows]
    outgoing_grads = spread[:, node_rows : node_rows + recv_total].astype(jnp.bfloat16)
    returned = lax.all_to_all(outgoing_grads, "dom", split_axis=1, concat_axis=1, tiled=True)
    grad_feats = grad_feats.at[:, send_list].add(returned.astype(jnp.float32))
    hub_grads = lax.psum_scatter(
        spread[:, node_rows + recv_total :].astype(jnp.bfloat16),
        "dom",
        scatter_dimension=1,
        tiled=True,
    ).astype(jnp.float32)
    grad_feats = grad_feats.at[:, hub_ids].add(hub_grads)
    return (
        activated,
        grad_feats.astype(jnp.bfloat16),
        grad_self * scale,
        grad_neigh * scale,
        grad_bias * scale,
    )


def solution(mesh):
    placed = (
        P("feat", "dom"),
        P("dom", None, None),
        P("dom"),
        P("dom"),
        P("dom"),
        P("dom", None, None),
        P("dom"),
        P("feat", None),
        P("feat", None),
        P("feat"),
        P("feat", "dom"),
    )
    return jax.shard_map(
        local,
        mesh=mesh,
        in_specs=placed,
        out_specs=(P("feat", "dom"), P("feat", "dom"), P("feat", None), P("feat", None), P("feat")),
        check_vma=False,
    )
```

profile of v0, /device:TPU:32, one launch (start us, length us, event | category | flops | bytes accessed | tf_op | source)
XLA Modules:
  0.0 442.0 jit_solution(11608947110800255752)
XLA Ops:
  7.2 0.7 all-gather.4.cloned.1.call-update
  7.9 0.7 compare_and_fusion
  8.6 0.8 reshape_squeeze.6
  9.4 1.9 copy.45
  11.4 6.2 %gather_fusion.2 = bf16[2048,16]{1,0:T(8,128)(2,1)S(1)} fusion(bf16[16,8192]{0,1:T(8,128)(2,1)S(1)} %copy.45, s32[2048]{0:T(1024)S(1)} %broadcast_clamp_fusion), kind=kCustom, calls=%fused_computation.2 | custom fusion | bytes 139264 | tf_op jit(solution)/shard_map/jit(_take)/gather | solution.py:92
  17.6 0.2 copy.46
  17.8 0.8 reshape.145
  18.6 11.4 %all-to-all-start = ((bf16[32,2,512]{2,1,0:T(2,128)(2,1)}), bf16[32,2,512]{2,1,0:T(2,128)(2,1)S(1)}, u32[]{:S(2)}, u32[]{:S(2)}) async-start(bf16[32,2,512]{2,1,0:T(2,128)(2,1)} %reshape.145), calls=%async_computation | async-start | bytes 131072 | tf_op jit(solution)/shard_map/all_to_all | solution.py:93
  30.0 0.5 copy-done.6
  30.5 0.7 gather_fusion.3
  32.0 49.8 %all_gather.21 = bf16[16,4096]{0,1:T(8,128)(2,1)S(1)} all-gather(bf16[16,128]{0,1:T(8,128)(2,1)S(1)} %select_bitcast_fusion), channel_id=1, replica_groups=mesh['dom'=32,'feat'=8] {'dom'}, dimensions={1}, use_global_device_ids=true | all-gather | bytes 135168 | tf_op jit(solution)/shard_map/all_gather | solution.py:95
  81.8 0.3 copy.49
  82.3 0.2 all_to_all.13
  82.8 10.3 %while.20 = (s32[]{:T(128)}, f32[64,16,128]{2,0,1:T(8,128)S(1)}, s32[]{:T(128)}, s32[320]{0:T(512)S(1)}, s32[]{:T(128)}, /*index=5*/s32[320]{0:T(512)S(1)}, bf16...) while((s32[]{:T(128)}, f32[64,16,128]{2,0,1:T(8,128)S(1)}, ...), condition=%wide.region_1.2_spmd, body=%wide.region_0.1_spmd.sunk | while | flops 134362432 | bytes 4986935 | solution.py:38
  82.9 0.7 add_compare_fusion.4
  83.7 0.6 gather_fusion
  84.3 2.8 fusion.64
  87.1 0.9 convolution_add_fusion.5
  88.0 0.7 add_compare_fusion.4
  88.8 0.6 gather_fusion
  89.4 2.8 fusion.64
  92.2 0.9 convolution_add_fusion.5
  93.2 0.9 copy.76
  94.1 13.2 %all_gather.18 = bf16[128,128]{1,0:T(8,128)(2,1)S(1)} all-gather(bf16[16,128]{1,0:T(8,128)(2,1)S(1)} %copy-done.3), channel_id=1, replica_groups=mesh['dom'=32,'feat'=8] {'feat'}, dimensions={0}, use_global_device_ids=true | all-gather | bytes 36864 | tf_op jit(solution)/shard_map/all_gather | solution.py:106
  107.3 12.8 %all_gather.20 = bf16[128,128]{1,0:T(8,128)(2,1)S(1)} all-gather(bf16[16,128]{1,0:T(8,128)(2,1)S(1)} %copy-done.2), channel_id=1, replica_groups=mesh['dom'=32,'feat'=8] {'feat'}, dimensions={0}, use_global_device_ids=true | all-gather | bytes 36864 | tf_op jit(solution)/shard_map/all_gather | solution.py:107
  120.1 2.1 fusion.32
  122.2 12.5 %all-gather.6.cloned.1.call-done = bf16[128,8192]{1,0:T(8,128)(2,1)} async-done(((bf16[16,8192]{1,0:T(8,128)(2,1)}), bf16[128,8192]{1,0:T(8,128)(2,1)}) %all-gather.6.cloned.1.call-update) | async-done | bytes 2097168 | tf_op jit(solution)/shard_map/all_gather | solution.py:105
  134.8 3.6 convert_reduce_fusion
  138.4 28.2 %all-gather.8.cloned.1.call-done = bf16[128,8192]{1,0:T(8,128)(2,1)} async-done(((bf16[16,8192]{1,0:T(8,128)(2,1)}), bf16[128,8192]{1,0:T(8,128)(2,1)}) %all-gather.8.cloned.1.call-update) | async-done | bytes 2097168 | tf_op jit(solution)/shard_map/all_gather | solution.py:119
  166.6 2.0 fusion.30
  168.7 10.0 %while.21 = (s32[]{:T(128)}, f32[112,16,128]{2,0,1:T(8,128)S(1)}, s32[]{:T(128)}, s32[320]{0:T(512)S(1)}, s32[]{:T(128)}, /*index=5*/s32[320]{0:T(512)S(1)}, bf1...) while((s32[]{:T(128)}, f32[112,16,128]{2,0,1:T(8,128)S(1)}, ...), condition=%wide.region_3.4_spmd, body=%wide.region_2.3_spmd.sunk | while | flops 209967424 | bytes 5773367 | solution.py:38
  168.7 0.7 add_compare_fusion.5
  169.5 0.6 gather_fusion.1
  170.2 2.2 fusion.69
  172.4 1.3 convolution_add_fusion.6
  173.7 0.7 add_compare_fusion.5
  174.5 0.6 gather_fusion.1
  175.2 2.2 fusion.69
  177.4 1.3 convolution_add_fusion.6
  178.7 0.3 copy.78
  179.0 0.3 copy.75
  179.3 0.6 slice.23
  179.9 0.7 slice.24
  180.6 1.7 all_to_all.14
  182.3 1.6 copy.79
  183.9 1.7 reshape.147
  185.5 21.9 %all-to-all-start.1 = ((bf16[32,2,512]{2,1,0:T(2,128)(2,1)}), bf16[32,2,512]{2,1,0:T(2,128)(2,1)}, u32[]{:S(2)}, u32[]{:S(2)}) async-start(bf16[32,2,512]{2,1,0:T(2,128)(2,1)} %reshape.147), calls=%async_computation.1 | async-start | bytes 131072 | tf_op jit(solution)/shard_map/all_to_all | solution.py:142
  207.4 0.2 reduce-scatter.4.cloned.1.call-start
  207.7 2.2 copy.58
  209.9 0.6 fusion.36
  210.6 0.7 convolution_bitcast_fusion.1
  211.2 137.6 %all-reduce = (f32[16,128]{1,0:T(8,128)}, f32[16,128]{1,0:T(8,128)}, f32[16]{0:T(128)}) all-reduce(f32[16,128]{1,0:T(8,128)S(1)} %convolution_bitcast_fusion.1, f32[16,128]{1,0:T(8,128)S(1)} %fusion.36, f32[16]{0:T(128)S(1)} %copy-done.8), channel_id=1, replica_groups=mesh['dom'=32,'feat'=8] {'dom'}, use_global_device_ids=true, to_apply=%region_7.8 | all-reduce | flops 4112 | bytes 32896 | tf_op jit(solution)/shard_map/psum | solution.py:123
  348.8 1.1 fusion.28
  349.9 0.6 broadcast_multiply_fusion
  350.5 2.6 copy.54
  353.1 0.5 broadcast_multiply_fusion.2
  353.7 1.0 reshape.148
  354.8 0.3 copy.55
  355.2 14.5 %scatter_fusion = f32[16,8192]{0,1:T(8,128)} fusion(f32[16,8192]{0,1:T(8,128)} %copy.54, s32[2048]{0:T(1024)S(1)} %bitcast.100, f32[2048,16]{1,0:T(8,128)S(1)} %copy.55), kind=kCustom, calls=%fused_computation.4 | custom fusion | flops 32768 | bytes 401408 | tf_op jit(solution)/shard_map/scatter-add | solution.py:143
  369.6 55.8 %reduce-scatter.4.cloned.1.call-done = bf16[128,16]{1,0:T(8,128)(2,1)} async-done(((bf16[4096,16]{1,0:T(8,128)(2,1)}), bf16[128,16]{1,0:T(8,128)(2,1)}) %reduce-scatter.4.cloned.1.call-update) | async-done | bytes 4112
  425.4 0.8 copy.59
  426.3 5.3 %scatter_fusion.1 = f32[16,8192]{0,1:T(8,128)} fusion(f32[16,8192]{0,1:T(8,128)} %scatter_fusion, s32[128]{0:T(128)S(1)} %copy-done.7, f32[128,16]{1,0:T(8,128)S(1)} %copy.56), kind=kCustom, calls=%fused_computation.5 | custom fusion | flops 2048 | bytes 25088 | tf_op jit(solution)/shard_map/scatter-add | solution.py:150
  431.6 2.4 convert_element_type.52
  434.0 1.4 copy.57
  (70 shorter events, 1.9 us)
Async XLA Ops:
  7.2 113.0 %all-gather.4.cloned.1.call-start = ((), (), s32[]{:S(2)}) async-start(), calls=%async_computation.3 | async-start | bytes 2359296 | tf_op jit(solution)/shard_map/all_gather | solution.py:104
  9.4 20.6 %copy-start.12 = (s32[128]{0:T(128)S(1)}, s32[128]{0:T(128)}, u32[]{:S(2)}) copy-start(s32[128]{0:T(128)} %param.21) | copy-start | bytes 1540
  17.6 64.9 %copy-start.1 = (bf16[16,8192]{1,0:T(8,128)(2,1)S(1)}, bf16[16,8192]{1,0:T(8,128)(2,1)}, u32[]{:S(2)}) copy-start(bf16[16,8192]{1,0:T(8,128)(2,1)} %param.15) | copy-start | bytes 786436
  18.6 63.5 %all-to-all-start = ((bf16[32,2,512]{2,1,0:T(2,128)(2,1)}), bf16[32,2,512]{2,1,0:T(2,128)(2,1)S(1)}, u32[]{:S(2)}, u32[]{:S(2)}) async-start(bf16[32,2,512]{2,1,0:T(2,128)(2,1)} %reshape.145), calls=%async_computation | async-start | bytes 131072 | tf_op jit(solution)/shard_map/all_to_all | solution.py:93
  29.9 104.8 %all-gather.6.cloned.1.call-start = ((), (), s32[]{:S(2)}) async-start(), calls=%async_computation.4 | async-start | bytes 2359296 | tf_op jit(solution)/shard_map/all_gather | solution.py:105
  30.0 0.5 copy-start.6
  82.1 0.7 copy-start.10
  82.1 0.7 copy-start.11
  82.8 11.3 %copy-start.3 = (bf16[16,128]{1,0:T(8,128)(2,1)S(1)}, bf16[16,128]{1,0:T(8,128)(2,1)}, u32[]{:S(2)}) copy-start(bf16[16,128]{1,0:T(8,128)(2,1)} %param.22) | copy-start | bytes 12292
  82.8 24.5 %copy-start.2 = (bf16[16,128]{1,0:T(8,128)(2,1)S(1)}, bf16[16,128]{1,0:T(8,128)(2,1)}, u32[]{:S(2)}) copy-start(bf16[16,128]{1,0:T(8,128)(2,1)} %param.23) | copy-start | bytes 12292
  93.1 41.6 %copy-start.9 = (bf16[16,8192]{1,0:T(8,128)(2,1)S(1)}, bf16[16,8192]{1,0:T(8,128)(2,1)}, u32[]{:S(2)}) copy-start(bf16[16,8192]{1,0:T(8,128)(2,1)} %param.25) | copy-start | bytes 786436
  93.1 41.6 %copy-start.13 = (f32[16]{0:T(128)S(1)}, f32[16]{0:T(128)}, u32[]{:S(2)}) copy-start(f32[16]{0:T(128)} %param.24) | copy-start | bytes 196
  94.1 72.5 %all-gather.8.cloned.1.call-start = ((), (), s32[]{:S(2)}) async-start(), calls=%async_computation.5 | async-start | bytes 2359296 | tf_op jit(solution)/shard_map/all_gather | solution.py:119
  179.3 30.6 %copy-start = (bf16[128,8192]{1,0:T(8,128)(2,1)S(1)}, bf16[128,8192]{1,0:T(8,128)(2,1)}, u32[]{:S(2)}) copy-start(bf16[128,8192]{1,0:T(8,128)(2,1)} %all-gather.8.cloned.1.call-done) | copy-start | bytes 6291460
  185.5 168.1 %all-to-all-start.1 = ((bf16[32,2,512]{2,1,0:T(2,128)(2,1)}), bf16[32,2,512]{2,1,0:T(2,128)(2,1)}, u32[]{:S(2)}, u32[]{:S(2)}) async-start(bf16[32,2,512]{2,1,0:T(2,128)(2,1)} %reshape.147), calls=%async_computation.1 | async-start | bytes 131072 | tf_op jit(solution)/shard_map/all_to_all | solution.py:142
  207.4 217.9 %reduce-scatter.4.cloned.1.call-start = ((), (), s32[]{:S(2)}) async-start(), calls=%async_computation.6 | async-start | bytes 1081344
  210.6 0.7 copy-start.8
  348.8 1.1 copy-start.4
  348.8 1.1 copy-start.5
  350.5 2.6 copy-start.14
  354.7 71.7 %copy-start.7 = (s32[128]{0:T(128)S(1)}, s32[128]{0:T(128)}, u32[]{:S(2)}) copy-start(s32[128]{0:T(128)} %copy-done.6) | copy-start | bytes 1540
Sparse Core Ops, SparseCore 0:
  9.9 30.2 all-gather.3
  94.2 40.5 all-gather.5
  138.5 28.0 all-gather.7
  211.8 213.5 reduce-scatter.3
where the time goes:
time: 445 us; the launch traced here: 442 us
  blocking collectives  213 us (48%)
  waiting for transfers between devices  97.2 us (22%)
  starting transfers between devices  33.6 us (8%)
  local copies, waits for them, and re-layouts  31.3 us (7%)
  other arithmetic  27.2 us (6%)
  matrix products  24.4 us (5%)
  between operations  14.8 us (3%)
    psum x1, blocking collectives, local(): lax.psum((grad_self, grad_neigh, grad_bias), 'dom')  138 us
    unnamed x5, waiting for transfers between devices  56.5 us
    all_gather x1, blocking collectives, local(): hub_table = lax.all_gather(hub_local, 'dom', axis=1, tiled=True)  49.8 us
    all_gather x1, waiting for transfers between devices, local(): grad_full = lax.all_gather(grad_linear, 'feat', axis=0, tiled=True)  28.2 us
    all_to_all x1, starting transfers between devices, local(): lax.all_to_all(outgoing_grads, 'dom', split_axis=1, concat_axis=1, tiled=...  21.9 us
    scatter-add x1, other arithmetic, local(): grad_feats = grad_feats.at[:, send_list].add(returned.astype(jnp.float32))  14.5 us
    all_gather x1, blocking collectives, local(): lax.all_gather(w_self, 'feat', axis=0, tiled=True)  13.2 us
    all_gather x1, blocking collectives, local(): lax.all_gather(w_neigh, 'feat', axis=0, tiled=True)  12.8 us
  transfers between devices with their start and end apart: 6, of which 3 were waited for; matrix products, arithmetic and copies ran while one was open for 11% of the time, Pallas kernels for 0%

commit v1 on v0

v1 whole, which is shorter than its diff:
```python
import functools
import math

import jax
import jax.numpy as jnp
from jax import lax
from jax.experimental import pallas as pl
from jax.experimental.pallas import tpu as pltpu
from jax.sharding import PartitionSpec as P

edge = 128
group = 8
chunk = 32
bf16 = jnp.bfloat16
f32 = jnp.float32
vmem = pl.BlockSpec(memory_space=pltpu.VMEM)
smem = pl.BlockSpec(memory_space=pltpu.SMEM)
hbm = pl.BlockSpec(memory_space=pl.ANY)


def params():
    return pltpu.CompilerParams(vmem_limit_bytes=48 * 1024 * 1024)


def lanes(rows):
    return lax.broadcasted_iota(jnp.int32, (rows, edge), 1)


def split(values, pieces):
    parts = []
    for _ in range(pieces):
        part = values.astype(bf16)
        parts.append(part)
        values = values - part.astype(f32)
    return parts


def column_block(column):
    hi, mid, lo = split(column, 3)
    lane = lanes(column.shape[0])
    block = jnp.where(lane == 0, hi.astype(f32), 0.0)
    block = jnp.where(lane == 1, mid.astype(f32), block)
    return jnp.where(lane == 2, lo.astype(f32), block)


def pick_kernel(index_ref, feats_ref, out_ref, blocks, picked):
    width, nodes = feats_ref.shape
    count = nodes // edge
    for b in range(count):
        blocks[b] = feats_ref[:, b * edge : (b + 1) * edge]
    whole = blocks[...].reshape(count * width, edge)
    sub = lax.broadcasted_iota(jnp.int32, (edge, edge), 0)

    def step(g, carry):
        index = index_ref[pl.ds(g, 1), :]
        place = index & (edge - 1)
        home = index >> 7
        hot = jnp.where(sub == place, 1.0, 0.0).astype(bf16)
        found = jnp.dot(whole, hot, preferred_element_type=f32)
        home = jnp.broadcast_to(home, (width, edge))
        total = jnp.zeros((width, edge), f32)
        for b in range(count):
            total = jnp.where(home == b, found[b * width : (b + 1) * width], total)
        picked[g] = total
        return carry

    groups = picked.shape[0]
    lax.fori_loop(0, groups, step, 0)
    lane = lanes(width)
    hub = picked[groups - 1].astype(bf16)
    for g in range(groups - 1):
        here = picked[g]
        turned = pltpu.roll(here, edge // 2, 1)
        for odd in range(2):
            first, second = (turned, here) if odd else (here, turned)
            out_ref[2 * g + odd, 0:width] = hub
            out_ref[2 * g + odd, width : 2 * width] = jnp.where(
                lane < edge // 2, first, second
            ).astype(bf16)


def pick(index, feats, domains):
    width, nodes = feats.shape
    groups = domains // 2 + 1
    return pl.pallas_call(
        pick_kernel,
        out_shape=jax.ShapeDtypeStruct((domains, 2 * width, edge), bf16),
        in_specs=[vmem, vmem],
        out_specs=vmem,
        scratch_shapes=[
            pltpu.VMEM((nodes // edge, width, edge), bf16),
            pltpu.VMEM((groups, width, edge), f32),
        ],
        compiler_params=params(),
        name="pick",
    )(index, feats)


def deal_kernel(feats_ref, cotangent_ref, self_ref, neigh_ref, bias_ref, out_ref):
    width, nodes = feats_ref.shape
    peers = out_ref.shape[0]
    share = nodes // peers
    bias = column_block(bias_ref[...]).astype(bf16)
    for k in range(peers):
        out_ref[k, :, 0:share] = feats_ref[:, k * share : (k + 1) * share]
        out_ref[k, :, share : 2 * share] = cotangent_ref[:, k * share : (k + 1) * share]
        out_ref[k, :, 2 * share : 2 * share + edge] = self_ref[...]
        out_ref[k, :, 2 * share + edge : 2 * share + 2 * edge] = neigh_ref[...]
        out_ref[k, :, 2 * share + 2 * edge : 2 * share + 3 * edge] = bias


def deal(feats, cotangent, w_self, w_neigh, bias, peers):
    width, nodes = feats.shape
    return pl.pallas_call(
        deal_kernel,
        out_shape=jax.ShapeDtypeStruct((peers, width, 2 * nodes // peers + 3 * edge), bf16),
        in_specs=[vmem] * 5,
        out_specs=vmem,
        compiler_params=params(),
        name="deal",
    )(feats, cotangent, w_self, w_neigh, bias[:, None])


def tile_walk(vals_ref, held, sems, count, visit):
    total = vals_ref.shape[0]
    chunks = total // chunk

    def copy(c):
        rows = pl.ds(c * chunk, chunk)
        return pltpu.make_async_copy(vals_ref.at[rows], held.at[rows], sems.at[c])

    live_chunks = (count + chunk - 1) // chunk

    def begin(c, carry):
        copy(c).start()
        return carry

    def finish(c, carry):
        copy(c).wait()
        first = c * chunk
        steps = (jnp.minimum(count - first, chunk) + group - 1) // group

        def some(i, inner):
            visit(first + i * group)
            return inner

        lax.fori_loop(0, steps, some, 0)
        return carry

    lax.fori_loop(0, live_chunks, begin, 0)
    return lambda: lax.fori_loop(0, live_chunks, finish, 0)


def gather_kernel(
    dst_ref, src_ref, count_ref, feats_ref, recv_ref, vals_ref, out_ref, ext, total, held, sems
):
    width, nodes = feats_ref.shape
    own = nodes // edge
    domains = recv_ref.shape[0]
    count = count_ref[0]

    def visit(first):
        products = []
        places = []
        for i in range(group):
            t = first + i
            products.append(
                lax.dot_general(
                    ext[src_ref[t]],
                    held[t],
                    (((1,), (1,)), ((), ())),
                    preferred_element_type=f32,
                )
            )
            places.append(jnp.where(t < count, dst_ref[t], own))
        for place, product in zip(places, products):
            total[place] += product

    walk = tile_walk(vals_ref, held, sems, count, visit)
    lane = lanes(width)
    for b in range(own):
        ext[b] = feats_ref[:, b * edge : (b + 1) * edge]
    for g in range(domains // 2):
        ext[own + g] = jnp.where(
            lane < edge // 2,
            recv_ref[2 * g, width : 2 * width].astype(f32),
            recv_ref[2 * g + 1, width : 2 * width].astype(f32),
        ).astype(bf16)
    for q in range(domains):
        ext[own + domains // 2 + q] = recv_ref[q, 0:width]
    total[...] = jnp.zeros_like(total)
    walk()
    peers = out_ref.shape[0]
    per = own // peers
    for b in range(own):
        col = (b % per) * edge
        out_ref[b // per, :, col : col + edge] = total[b].astype(bf16)


def gather(dst, src, count, feats, recv, vals, peers):
    width, nodes = feats.shape
    domains = recv.shape[0]
    own = nodes // edge
    tiles = vals.shape[0]
    return pl.pallas_call(
        gather_kernel,
        out_shape=jax.ShapeDtypeStruct((peers, width, nodes // peers), bf16),
        in_specs=[smem, smem, smem, vmem, vmem, hbm],
        out_specs=vmem,
        scratch_shapes=[
            pltpu.VMEM((own + domains // 2 + domains, width, edge), bf16),
            pltpu.VMEM((own + 1, width, edge), f32),
            pltpu.VMEM((tiles, edge, edge), bf16),
            pltpu.SemaphoreType.DMA((tiles // chunk,)),
        ],
        compiler_params=params(),
        name="gather",
    )(dst, src, count, feats, recv, vals)


def spread_kernel(
    dst_ref, src_ref, count_ref, grads_ref, vals_ref, out_ref, own_ref, blocks, total, held, sems
):
    peers, width, _ = grads_ref.shape
    own = own_ref.shape[0]
    per = own // peers
    share = per * edge
    domains = out_ref.shape[0]
    far = own + domains // 2
    spare = far + domains
    count = count_ref[0]

    def visit(first):
        products = []
        places = []
        for i in range(group):
            t = first + i
            products.append(
                jnp.dot(blocks[dst_ref[t]], held[t], preferred_element_type=f32)
            )
            places.append(jnp.where(t < count, src_ref[t], spare))
        for place, product in zip(places, products):
            total[place] += product

    walk = tile_walk(vals_ref, held, sems, count, visit)
    for b in range(own):
        col = (b % per) * edge
        blocks[b] = grads_ref[b // per, :, col : col + edge]
    total[...] = jnp.zeros_like(total)

    def summed(place):
        return jnp.sum(grads_ref[:, :, share + place * edge : share + (place + 1) * edge].astype(f32), axis=0)

    grad_self = (summed(0) + summed(1)).astype(bf16)
    grad_neigh = (summed(2) + summed(3)).astype(bf16)
    grad_bias = column_block(jnp.sum(summed(4), axis=1, keepdims=True))
    walk()
    own_ref[...] = total[0:own]
    lane = lanes(width)
    grad_bias = pltpu.roll(grad_bias, edge // 2, 1)
    for g in range(domains // 2):
        here = total[own + g]
        for odd in range(2):
            q = 2 * g + odd
            mine = pltpu.roll(here, edge // 2, 1) if odd else here
            out_ref[q, 0:width] = total[far + q].astype(bf16)
            out_ref[q, width : 2 * width] = jnp.where(lane < edge // 2, mine, grad_bias).astype(bf16)
            out_ref[q, 2 * width : 3 * width] = grad_self
            out_ref[q, 3 * width : 4 * width] = grad_neigh


def spread(dst, src, count, grads, vals, domains, nodes):
    _, width, _ = grads.shape
    own = nodes // edge
    tiles = vals.shape[0]
    return pl.pallas_call(
        spread_kernel,
        out_shape=(
            jax.ShapeDtypeStruct((domains, 4 * width, edge), bf16),
            jax.ShapeDtypeStruct((own, width, edge), f32),
        ),
        in_specs=[smem, smem, smem, vmem, hbm],
        out_specs=(vmem, vmem),
        scratch_shapes=[
            pltpu.VMEM((own, width, edge), bf16),
            pltpu.VMEM((own + domains // 2 + domains + 1, width, edge), f32),
            pltpu.VMEM((tiles, edge, edge), bf16),
            pltpu.SemaphoreType.DMA((tiles // chunk,)),
        ],
        compiler_params=params(),
        name="spread",
    )(dst, src, count, grads, vals)


def layer_kernel(dealt_ref, agg_ref, near_ref, late_ref):
    peers, width, share = agg_ref.shape
    rows = peers * width

    def part(start, size):
        return dealt_ref[:, :, start : start + size].reshape(rows, size)

    feats = part(0, share)
    cotangent = part(share, share)
    w_self = part(2 * share, edge)
    w_neigh = part(2 * share + edge, edge)
    bias = jnp.sum(part(2 * share + 2 * edge, edge).astype(f32), axis=1, keepdims=True)
    aggregate = agg_ref[...].reshape(rows, share)
    first = (((0,), (0,)), ((), ()))
    last = (((1,), (1,)), ((), ()))
    linear = lax.dot_general(w_self, feats, first, preferred_element_type=f32)
    linear = linear + lax.dot_general(w_neigh, aggregate, first, preferred_element_type=f32)
    linear = linear + bias
    logistic = jax.nn.sigmoid(linear)
    late_ref[:, :, 0:share] = (linear * logistic).astype(bf16).reshape(peers, width, share)
    slope = logistic * (1.0 + linear * (1.0 - logistic))
    grad = (cotangent.astype(f32) * slope).astype(bf16)
    near_ref[:, :, 0:share] = (
        jnp.dot(w_neigh, grad, preferred_element_type=f32).astype(bf16).reshape(peers, width, share)
    )
    late_ref[:, :, share : 2 * share] = (
        jnp.dot(w_self, grad, preferred_element_type=f32).astype(bf16).reshape(peers, width, share)
    )
    grad_self = lax.dot_general(feats, grad, last, preferred_element_type=f32)
    grad_neigh = lax.dot_general(aggregate, grad, last, preferred_element_type=f32)
    grad_bias = column_block(jnp.sum(grad.astype(f32), axis=1, keepdims=True)).astype(bf16)
    pieces = split(grad_self, 2) + split(grad_neigh, 2) + [grad_bias]
    for place, piece in enumerate(pieces):
        near_ref[:, :, share + place * edge : share + (place + 1) * edge] = piece.reshape(
            peers, width, edge
        )


def layer(dealt, agg):
    peers, width, share = agg.shape
    return pl.pallas_call(
        layer_kernel,
        out_shape=(
            jax.ShapeDtypeStruct((peers, width, share + 5 * edge), bf16),
            jax.ShapeDtypeStruct((peers, width, 2 * share), bf16),
        ),
        in_specs=[vmem, vmem],
        out_specs=(vmem, vmem),
        compiler_params=params(),
        name="layer",
    )(dealt, agg)


def settle_kernel(
    scale,
    index_ref,
    recv_ref,
    late_ref,
    own_ref,
    act_ref,
    feats_ref,
    self_ref,
    neigh_ref,
    bias_ref,
    values,
    marked,
    placed,
):
    domains = recv_ref.shape[0]
    peers, width, share = late_ref.shape
    share = share // 2
    own = own_ref.shape[0]
    per = own // peers
    pairs = domains // 2
    lane = lanes(width)

    def over(start):
        return jnp.sum(recv_ref[:, start : start + width].astype(f32), axis=0)

    hub = over(0)
    self_ref[...] = over(2 * width) * scale
    neigh_ref[...] = over(3 * width) * scale
    tail = jnp.where(lane >= edge // 2, over(width), 0.0)
    bias_ref[...] = jnp.sum(tail, axis=1, keepdims=True) * scale
    for g in range(pairs):
        here = recv_ref[2 * g, width : 2 * width].astype(f32)
        other = pltpu.roll(recv_ref[2 * g + 1, width : 2 * width].astype(f32), edge // 2, 1)
        values[g] = jnp.where(lane < edge // 2, here, other)
    for k, piece in enumerate(split(hub, 3)):
        values[pairs + k] = piece.astype(f32)
    sub = lax.broadcasted_iota(jnp.int32, (edge, edge), 0)
    placed[...] = jnp.zeros_like(placed)

    def step(g, carry):
        index = index_ref[pl.ds(jnp.minimum(g, pairs), 1), :]
        place = index & (edge - 1)
        home = jnp.broadcast_to(index >> 7, (width, edge))
        hot = jnp.where(sub == place, 1.0, 0.0).astype(bf16)
        value = values[g]
        for b in range(own):
            marked[b] = jnp.where(home == b, value, 0.0).astype(bf16)
        placed[...] += lax.dot_general(
            marked[...].reshape(own * width, edge),
            hot,
            (((1,), (1,)), ((), ())),
            preferred_element_type=f32,
        )
        return carry

    lax.fori_loop(0, pairs + 3, step, 0)
    for k in range(peers):
        act_ref[:, k * share : (k + 1) * share] = late_ref[k, :, 0:share]
    for b in range(own):
        col = share + (b % per) * edge
        feats_ref[:, b * edge : (b + 1) * edge] = (
            late_ref[b // per, :, col : col + edge].astype(f32)
            + own_ref[b]
            + placed[b * width : (b + 1) * width]
        ).astype(bf16)


def settle(index, recv, late, own, scale):
    peers, width, share = late.shape
    nodes = own.shape[0] * edge
    domains = recv.shape[0]
    return pl.pallas_call(
        functools.partial(settle_kernel, scale),
        out_shape=(
            jax.ShapeDtypeStruct((width, nodes), bf16),
            jax.ShapeDtypeStruct((width, nodes), bf16),
            jax.ShapeDtypeStruct((width, edge), f32),
            jax.ShapeDtypeStruct((width, edge), f32),
            jax.ShapeDtypeStruct((width, 1), f32),
        ),
        in_specs=[vmem] * 4,
        out_specs=(vmem,) * 5,
        scratch_shapes=[
            pltpu.VMEM((domains // 2 + 3, width, edge), f32),
            pltpu.VMEM((own.shape[0], width, edge), bf16),
            pltpu.VMEM((own.shape[0] * width, edge), f32),
        ],
        compiler_params=params(),
        name="settle",
    )(index, recv, late, own)


def swap(values, axis):
    return lax.all_to_all(values, axis, split_axis=0, concat_axis=0, tiled=True)


def local(
    feats,
    tile_vals,
    tile_dst,
    tile_src,
    tile_count,
    send_rows,
    hub_ids,
    w_self,
    w_neigh,
    bias,
    cotangent,
):
    nodes = feats.shape[1]
    domains = lax.axis_size("dom")
    peers = lax.axis_size("feat")
    index = jnp.concatenate([send_rows.reshape(domains // 2, edge), hub_ids.reshape(1, edge)])
    recv = swap(pick(index, feats, domains), "dom")
    dealt = swap(deal(feats, cotangent, w_self, w_neigh, bias, peers), "feat")
    agg = swap(gather(tile_dst, tile_src, tile_count, feats, recv, tile_vals, peers), "feat")
    near, late = layer(dealt, agg)
    near = swap(near, "feat")
    late = swap(late, "feat")
    back, own = spread(tile_dst, tile_src, tile_count, near, tile_vals, domains, nodes)
    back = swap(back, "dom")
    scale = 1.0 / math.sqrt(nodes * domains)
    act, grad_feats, grad_self, grad_neigh, grad_bias = settle(index, back, late, own, scale)
    return act, grad_feats, grad_self, grad_neigh, grad_bias[:, 0]


def solution(mesh):
    placed = (
        P("feat", "dom"),
        P("dom", None, None),
        P("dom"),
        P("dom"),
        P("dom"),
        P("dom", None, None),
        P("dom"),
        P("feat", None),
        P("feat", None),
        P("feat"),
        P("feat", "dom"),
    )
    return jax.shard_map(
        local,
        mesh=mesh,
        in_specs=placed,
        out_specs=(P("feat", "dom"), P("feat", "dom"), P("feat", None), P("feat", None), P("feat")),
        check_vma=False,
    )
```

time: 445 us -> 119 us (0.27)
  blocking collectives: 213 us -> 49.5 us
  waiting for transfers between devices: 97.2 us -> 15.9 us
  other arithmetic: 27.2 us -> 1.29 us
  matrix products: 24.4 us -> 0 us
  local copies, waits for them, and re-layouts: 31.3 us -> 8.07 us
  Pallas kernels: 0 us -> 22.9 us
  starting transfers between devices: 33.6 us -> 19.1 us
  between operations: 14.8 us -> 1.37 us
    psum x1 -> x0, blocking collectives: 138 us -> none  [local(): lax.psum((grad_self, grad_neigh, grad_bias), 'dom')]
    all_gather x3 -> x0, blocking collectives: 75.7 us -> none  [the longest x1 49.8 us: local(): hub_table = lax.all_gather(hub_local, 'dom', axis=1, tiled=True)]
    unnamed x5 -> x0, waiting for transfers between devices: 56.5 us -> none
    all_to_all x0 -> x3, blocking collectives: none -> 49.5 us  [swap(): return lax.all_to_all(values, axis, split_axis=0, concat_axis=0, tiled=True)]
    all_gather x3 -> x0, waiting for transfers between devices: 40.7 us -> none  [the longest x1 28.2 us: local(): grad_full = lax.all_gather(grad_linear, 'feat', axis=0, tiled=True)]
    dot_general x14 -> x0, matrix products: 24.4 us -> none  [the longest x2 5.54 us: step_fn(): jnp.einsum('gfs,gds->gfd', picked, tile_block, preferred_element_type=jnp...]
    pallas_call x0 -> x6, Pallas kernels: none -> 22.9 us  [the longest x1 5.51 us: gather(): pl.pallas_call(gather_kernel, out_shape=jax.ShapeDtypeStruct((peers, widt...]
    scatter-add x2 -> x0, other arithmetic: 19.7 us -> none  [the longest x1 14.5 us: local(): grad_feats = grad_feats.at[:, send_list].add(returned.astype(jnp.float32))]
  transfers between devices with their start and end apart: 6 -> 3, of which waited for: 3 -> 3; matrix products, arithmetic and copies ran while one was open for 11% -> 1% of each run, Pallas kernels for 0% -> 9%
where the time goes in v1:
time: 119 us; the launch traced here: 118 us
  blocking collectives  49.5 us (42%)
  Pallas kernels  22.9 us (19%)
  starting transfers between devices  19.1 us (16%)
  waiting for transfers between devices  15.9 us (13%)
  local copies, waits for them, and re-layouts  8.07 us (7%)
  between operations  1.37 us (1%)
  other arithmetic  1.29 us (1%)
    all_to_all x3, blocking collectives, swap(): return lax.all_to_all(values, axis, split_axis=0, concat_axis=0, tiled=True)  49.5 us
    all_to_all x3, starting transfers between devices, swap(): return lax.all_to_all(values, axis, split_axis=0, concat_axis=0, tiled=True)  19.1 us
    all_to_all x3, waiting for transfers between devices, swap(): return lax.all_to_all(values, axis, split_axis=0, concat_axis=0, tiled=True)  15.9 us
    unnamed x20, local copies, waits for them, and re-layouts  6.54 us
    pallas_call x1, Pallas kernels, gather(): pl.pallas_call(gather_kernel, out_shape=jax.ShapeDtypeStruct((peers, widt...  5.51 us
    pallas_call x1, Pallas kernels, settle(): pl.pallas_call(functools.partial(settle_kernel, scale), out_shape=(jax.Sh...  5.48 us
    pallas_call x1, Pallas kernels, pick(): pl.pallas_call(pick_kernel, out_shape=jax.ShapeDtypeStruct((domains, 2 *...  4.84 us
    pallas_call x1, Pallas kernels, spread(): pl.pallas_call(spread_kernel, out_shape=(jax.ShapeDtypeStruct((domains, 4...  4.64 us
  transfers between devices with their start and end apart: 3, of which 3 were waited for; matrix products, arithmetic and copies ran while one was open for 1% of the time, Pallas kernels for 9%

profile of v1, /device:TPU:32, one launch (start us, length us, event | category | flops | bytes accessed | tf_op | source)
XLA Modules:
  0.0 118.1 jit_solution(21576054897738642)
XLA Ops:
  0.6 0.0 copy-start.7
  0.6 0.0 copy-start.5
  0.7 0.8 reshape.16
  1.5 0.7 pad_add_fusion.index_ref
  2.1 0.0 copy-start
  2.1 0.9 copy-done
  3.1 4.8 %pick.1 = bf16[32,32,128]{2,1,0:T(8,128)(2,1)} custom-call(s32[17,128]{1,0:T(8,128)S(1)} %pad_add_fusion.index_ref, bf16[16,8192]{1,0:T(8,128)(2,1)S(1)} %copy-done), custom_call_target="tpu_custom_call" | custom-call | tf_op jit(solution)/shard_map/pick/pallas_call | solution.py:85
  7.9 11.4 %all-to-all-start.1 = ((bf16[32,32,128]{2,1,0:T(8,128)(2,1)}), bf16[32,32,128]{2,1,0:T(8,128)(2,1)S(1)}, u32[]{:S(2)}, u32[]{:S(2)}) async-start(bf16[32,32,128]{2,1,0:T(8,128)(2,1)} %pick.1), calls=%async_computation.1 | async-start | bytes 524288 | tf_op jit(solution)/shard_map/all_to_all | solution.py:442
  19.3 0.7 copy.17.bias_ref
  20.0 0.0 copy-start.1
  20.0 0.9 copy-done.1
  21.0 0.0 copy-start.3
  21.0 0.9 copy-done.3
  21.9 0.0 copy-start.8
  21.9 0.7 copy-done.8
  22.6 0.0 copy-start.9
  22.6 0.7 copy-done.9
  23.3 0.9 deal.1
  24.2 7.4 %all-to-all-done.1.recv_ref = bf16[32,32,128]{2,1,0:T(8,128)(2,1)S(1)} async-done(((bf16[32,32,128]{2,1,0:T(8,128)(2,1)}), bf16[32,32,128]{2,1,0:T(8,128)(2,1)S(1)}, u32[]{:S(2)}, u32[]{:S(2)}) %all-to-all-start.1) | async-done | bytes 262176 | tf_op jit(solution)/shard_map/all_to_all | solution.py:442
  31.6 4.3 %all-to-all-start = ((bf16[8,16,2432]{2,1,0:T(8,128)(2,1)}), bf16[8,16,2432]{2,1,0:T(8,128)(2,1)S(1)}, u32[]{:S(2)}, u32[]{:S(2)}) async-start(bf16[8,16,2432]{2,1,0:T(8,128)(2,1)} %deal.1), calls=%async_computation | async-start | bytes 1245184 | tf_op jit(solution)/shard_map/all_to_all | solution.py:442
  36.5 0.0 copy-start.2
  36.5 0.9 copy-done.2
  37.5 0.0 copy-start.4
  37.5 0.7 copy-done.4
  38.2 0.0 copy-start.6
  38.2 0.7 copy-done.6
  38.8 5.5 %gather.1 = bf16[8,16,1024]{2,1,0:T(8,128)(2,1)S(1)} custom-call(s32[320]{0:T(512)S(1)} %copy-done.4, s32[320]{0:T(512)S(1)} %copy-done.6, s32[1]{0:T(128)S(6)} %copy.18.count_ref, bf16[16,8192]{1,0:T(8,128)(2,1)S(1)} %copy-done.2, bf16[32,32,128]{2,1,0:T(8,128)(2,1)S(1)} %all-to-all-done.1.recv_ref, bf16[320,128,128]{2,1,0:T(8,128)(2,1)} %vals_ref.3), custom_call_target="tpu_custom_call" | custom-call | tf_op jit(solution)/shard_map/gather/pallas_call | solution.py:205
  44.4 2.9 %all-to-all-done.dealt_ref = bf16[8,16,2432]{2,1,0:T(8,128)(2,1)S(1)} async-done(((bf16[8,16,2432]{2,1,0:T(8,128)(2,1)}), bf16[8,16,2432]{2,1,0:T(8,128)(2,1)S(1)}, u32[]{:S(2)}, u32[]{:S(2)}) %all-to-all-start) | async-done | bytes 622624 | tf_op jit(solution)/shard_map/all_to_all | solution.py:442
  47.3 9.9 %all_to_all.30.agg_ref = bf16[8,16,1024]{2,1,0:T(8,128)(2,1)S(1)} all-to-all(bf16[8,16,1024]{2,1,0:T(8,128)(2,1)S(1)} %gather.1), channel_id=1, replica_groups=mesh['dom'=32,'feat'=8] {'feat'}, dimensions={0} | all-to-all | bytes 524288 | tf_op jit(solution)/shard_map/all_to_all | solution.py:442
  57.2 1.5 %layer.1 = (bf16[8,16,1664]{2,1,0:T(8,128)(2,1)S(1)}, bf16[8,16,2048]{2,1,0:T(8,128)(2,1)}) custom-call(bf16[8,16,2432]{2,1,0:T(8,128)(2,1)S(1)} %all-to-all-done.dealt_ref, bf16[8,16,1024]{2,1,0:T(8,128)(2,1)S(1)} %all_to_all.30.agg_ref), custom_call_target="tpu_custom_call" | custom-call | tf_op jit(solution)/shard_map/layer/pallas_call | solution.py:335
  58.7 11.7 %all_to_all.31.grads_ref = bf16[8,16,1664]{2,1,0:T(8,128)(2,1)S(1)} all-to-all(bf16[8,16,1664]{2,1,0:T(8,128)(2,1)S(1)} %get-tuple-element.14), channel_id=1, replica_groups=mesh['dom'=32,'feat'=8] {'feat'}, dimensions={0} | all-to-all | bytes 851968 | tf_op jit(solution)/shard_map/all_to_all | solution.py:442
  70.4 3.5 %all-to-all-start.5 = ((bf16[8,16,2048]{2,1,0:T(8,128)(2,1)}), bf16[8,16,2048]{2,1,0:T(8,128)(2,1)S(1)}, u32[]{:S(2)}, u32[]{:S(2)}) async-start(bf16[8,16,2048]{2,1,0:T(8,128)(2,1)} %get-tuple-element.16), calls=%async_computation.5 | async-start | bytes 1048576 | tf_op jit(solution)/shard_map/all_to_all | solution.py:442
  73.9 0.0 copy-done.7
  73.9 0.0 copy-done.5
  73.9 4.6 %spread.1 = (bf16[32,64,128]{2,1,0:T(8,128)(2,1)S(1)}, f32[64,16,128]{2,1,0:T(8,128)S(1)}) custom-call(s32[320]{0:T(512)S(1)} %copy-done.5, s32[320]{0:T(512)S(1)} %copy-done.7, s32[1]{0:T(128)S(6)} %copy.18.count_ref, bf16[8,16,1664]{2,1,0:T(8,128)(2,1)S(1)} %all_to_all.31.grads_ref, bf16[320,128,128]{2,1,0:T(8,128)(2,1)} %vals_ref.3), custom_call_target="tpu_custom_call" | custom-call | tf_op jit(solution)/shard_map/spread/pallas_call | solution.py:276
  78.6 5.6 %all-to-all-done.5.late_ref = bf16[8,16,2048]{2,1,0:T(8,128)(2,1)S(1)} async-done(((bf16[8,16,2048]{2,1,0:T(8,128)(2,1)}), bf16[8,16,2048]{2,1,0:T(8,128)(2,1)S(1)}, u32[]{:S(2)}, u32[]{:S(2)}) %all-to-all-start.5) | async-done | bytes 524320 | tf_op jit(solution)/shard_map/all_to_all | solution.py:442
  84.2 27.9 %all_to_all.32.recv_ref = bf16[32,64,128]{2,1,0:T(8,128)(2,1)S(1)} all-to-all(bf16[32,64,128]{2,1,0:T(8,128)(2,1)S(1)} %get-tuple-element.15), channel_id=1, replica_groups=mesh['dom'=32,'feat'=8] {'dom'}, dimensions={0} | all-to-all | bytes 1048576 | tf_op jit(solution)/shard_map/all_to_all | solution.py:442
  112.0 5.5 %settle.1 = (bf16[16,8192]{1,0:T(8,128)(2,1)}, bf16[16,8192]{1,0:T(8,128)(2,1)}, f32[16,128]{1,0:T(8,128)}, f32[16,128]{1,0:T(8,128)}, f32[16,1]{1,0:T(8,128)S(1)}) custom-call(s32[17,128]{1,0:T(8,128)S(1)} %pad_add_fusion.index_ref, bf16[32,64,128]{2,1,0:T(8,128)(2,1)S(1)} %all_to_all.32.recv_ref, bf16[8,16,2048]{2,1,0:T(8,128)(2,1)S(1)} %all-to-all-done.5.late_ref, ...), custom_call_target="tpu_custom_call" | custom-call | tf_op jit(solution)/shard_map/settle/pallas_call | solution.py:420
  117.5 0.6 reduce
Async XLA Ops:
  0.6 73.3 %copy-start.7 = (s32[320]{0:T(512)S(1)}, s32[320]{0:T(512)}, u32[]{:S(2)}) copy-start(s32[320]{0:T(512)} %src_ref.3) | copy-start | bytes 3844
  0.6 73.3 %copy-start.5 = (s32[320]{0:T(512)S(1)}, s32[320]{0:T(512)}, u32[]{:S(2)}) copy-start(s32[320]{0:T(512)} %dst_ref.3) | copy-start | bytes 3844
  2.1 0.9 copy-start
  7.9 23.7 %all-to-all-start.1 = ((bf16[32,32,128]{2,1,0:T(8,128)(2,1)}), bf16[32,32,128]{2,1,0:T(8,128)(2,1)S(1)}, u32[]{:S(2)}, u32[]{:S(2)}) async-start(bf16[32,32,128]{2,1,0:T(8,128)(2,1)} %pick.1), calls=%async_computation.1 | async-start | bytes 524288 | tf_op jit(solution)/shard_map/all_to_all | solution.py:442
  20.0 0.9 copy-start.1
  21.0 0.9 copy-start.3
  21.9 0.7 copy-start.8
  22.6 0.7 copy-start.9
  31.6 15.7 %all-to-all-start = ((bf16[8,16,2432]{2,1,0:T(8,128)(2,1)}), bf16[8,16,2432]{2,1,0:T(8,128)(2,1)S(1)}, u32[]{:S(2)}, u32[]{:S(2)}) async-start(bf16[8,16,2432]{2,1,0:T(8,128)(2,1)} %deal.1), calls=%async_computation | async-start | bytes 1245184 | tf_op jit(solution)/shard_map/all_to_all | solution.py:442
  36.5 1.0 copy-start.2
  37.5 0.7 copy-start.4
  38.2 0.7 copy-start.6
  70.4 13.8 %all-to-all-start.5 = ((bf16[8,16,2048]{2,1,0:T(8,128)(2,1)}), bf16[8,16,2048]{2,1,0:T(8,128)(2,1)S(1)}, u32[]{:S(2)}, u32[]{:S(2)}) async-start(bf16[8,16,2048]{2,1,0:T(8,128)(2,1)} %get-tuple-element.16), calls=%async_computation.5 | async-start | bytes 1048576 | tf_op jit(solution)/shard_map/all_to_all | solution.py:442

commit v2 on v1

v2 whole, which is shorter than its diff:
```python
import functools
import math

import jax
import jax.numpy as jnp
from jax import lax
from jax.experimental import pallas as pl
from jax.experimental.pallas import tpu as pltpu
from jax.sharding import PartitionSpec as P

edge = 128
span = 256
group = 32
bf16 = jnp.bfloat16
f32 = jnp.float32
vmem = pl.BlockSpec(memory_space=pltpu.VMEM)
smem = pl.BlockSpec(memory_space=pltpu.SMEM)
hbm = pl.BlockSpec(memory_space=pl.ANY)


def params(mib):
    return pltpu.CompilerParams(vmem_limit_bytes=mib * 1024 * 1024)


def far_off(*values):
    return [pltpu.with_memory_space_constraint(value, pltpu.HBM) for value in values]


def lanes(rows):
    return lax.broadcasted_iota(jnp.int32, (rows, edge), 1)


def split(values, pieces):
    parts = []
    for _ in range(pieces):
        part = values.astype(bf16)
        parts.append(part)
        values = values - part.astype(f32)
    return parts


def column_block(column):
    hi, mid, lo = split(column, 3)
    lane = lanes(column.shape[0])
    block = jnp.where(lane == 0, hi.astype(f32), 0.0)
    block = jnp.where(lane == 1, mid.astype(f32), block)
    return jnp.where(lane == 2, lo.astype(f32), block)


def pick_kernel(
    rows_ref, hub_ref, feats_ref, out_ref, hot_ref, home_ref, near, hub, wide, index, blocks, picked, sems
):
    width, nodes = feats_ref.shape
    count = nodes // span
    pairs = rows_ref.shape[0] // 2
    half = edge // 2
    copies = [
        pltpu.make_async_copy(feats_ref, near, sems.at[0]),
        pltpu.make_async_copy(rows_ref, wide, sems.at[1]),
        pltpu.make_async_copy(hub_ref, hub, sems.at[2]),
    ]
    for copy in copies:
        copy.start()
    copies[1].wait()
    copies[2].wait()
    lane = lanes(1)
    for g in range(pairs):
        row = jnp.concatenate([wide[2 * g : 2 * g + 1, :], wide[2 * g + 1 : 2 * g + 2, :]], axis=1)
        index[g : g + 1, :] = row
    index[pairs : pairs + 1, :] = hub[...].reshape(1, edge)
    home_ref[...] = index[...] >> 8
    copies[0].wait()
    for b in range(count):
        blocks[b] = near[:, b * span : (b + 1) * span]
    sub = lax.broadcasted_iota(jnp.int32, (span, edge), 0)

    def step(g, carry):
        place = index[pl.ds(g, 1), :] & (span - 1)
        home = jnp.broadcast_to(home_ref[pl.ds(g, 1), :], (width, edge))
        hot = jnp.where(sub == place, 1.0, 0.0).astype(bf16)
        hot_ref[g] = hot
        found = jnp.dot(blocks[...].reshape(count * width, span), hot, preferred_element_type=f32)
        total = found[0:width]
        for b in range(1, count):
            total = jnp.where(home == b, found[b * width : (b + 1) * width], total)
        picked[g] = total
        return carry

    lax.fori_loop(0, pairs, step, 0, unroll=4)
    step(pairs, 0)
    lane = lanes(width)
    mine = picked[pairs].astype(bf16)
    for g in range(pairs):
        here = picked[g]
        turned = pltpu.roll(here, half, 1)
        for odd in range(2):
            first, second = (turned, here) if odd else (here, turned)
            out_ref[2 * g + odd, 0:width] = mine
            out_ref[2 * g + odd, width : 2 * width] = jnp.where(lane < half, first, second).astype(
                bf16
            )


def pick(rows, hub_ids, feats):
    width, nodes = feats.shape
    domains, slots = rows.shape
    groups = domains // 2 + 1
    return pl.pallas_call(
        pick_kernel,
        out_shape=(
            jax.ShapeDtypeStruct((domains, 2 * width, edge), bf16),
            jax.ShapeDtypeStruct((groups, span, edge), bf16),
            jax.ShapeDtypeStruct((groups, edge), jnp.int32),
        ),
        in_specs=[hbm, hbm, hbm],
        out_specs=(vmem, vmem, vmem),
        scratch_shapes=[
            pltpu.VMEM((width, nodes), bf16),
            pltpu.VMEM((edge,), jnp.int32),
            pltpu.VMEM((domains, slots), jnp.int32),
            pltpu.VMEM((groups, edge), jnp.int32),
            pltpu.VMEM((nodes // span, width, span), bf16),
            pltpu.VMEM((groups, width, edge), f32),
            pltpu.SemaphoreType.DMA((3,)),
        ],
        compiler_params=params(32),
        name="pick",
    )(*far_off(rows, hub_ids, feats))


def deal_kernel(feats_ref, cotangent_ref, self_ref, neigh_ref, bias_ref, *rest):
    peers = len(rest) - 4
    outs, (w_self, w_neigh, bias, sems) = rest[:peers], rest[peers:]
    width, nodes = feats_ref.shape
    share = nodes // peers
    here = lax.axis_index("feat")
    small = [
        pltpu.make_async_copy(self_ref, w_self, sems.at[0]),
        pltpu.make_async_copy(neigh_ref, w_neigh, sems.at[1]),
        pltpu.make_async_copy(bias_ref, bias, sems.at[2]),
    ]
    large = []
    for k, out in enumerate(outs):
        there = pl.ds(pl.multiple_of((here ^ k) * share, share), share)
        for place, ref in enumerate((feats_ref, cotangent_ref)):
            large.append(
                pltpu.make_async_copy(
                    ref.at[:, there],
                    out.at[:, place * share : (place + 1) * share],
                    sems.at[3 + 2 * k + place],
                )
            )
    for copy in small + large:
        copy.start()
    for copy in small:
        copy.wait()
    square = (width, width)
    diagonal = lax.broadcasted_iota(jnp.int32, square, 0) == lax.broadcasted_iota(
        jnp.int32, square, 1
    )
    spread_bias = jnp.broadcast_to(bias[...].reshape(1, width), square)
    column = jnp.sum(jnp.where(diagonal, spread_bias, 0.0), axis=1, keepdims=True)
    block = column_block(column).astype(bf16)
    for out in outs:
        out[:, 2 * share : 2 * share + edge] = w_self[...]
        out[:, 2 * share + edge : 2 * share + 2 * edge] = w_neigh[...]
        out[:, 2 * share + 2 * edge : 2 * share + 3 * edge] = block
    for copy in large:
        copy.wait()


def deal(feats, cotangent, w_self, w_neigh, bias, peers):
    width, nodes = feats.shape
    part = jax.ShapeDtypeStruct((width, 2 * nodes // peers + 3 * edge), bf16)
    return pl.pallas_call(
        deal_kernel,
        out_shape=(part,) * peers,
        in_specs=[hbm] * 5,
        out_specs=(vmem,) * peers,
        scratch_shapes=[
            pltpu.VMEM((width, edge), bf16),
            pltpu.VMEM((width, edge), bf16),
            pltpu.VMEM((width,), f32),
            pltpu.SemaphoreType.DMA((3 + 2 * peers,)),
        ],
        compiler_params=params(32),
        name="deal",
    )(*far_off(feats, cotangent, w_self, w_neigh, bias))


def products_of(lefts, tiles, turned):
    results = []
    for i in range(0, len(tiles), 2):
        left = jnp.concatenate([lefts[i], lefts[i + 1]], axis=0)
        right = jnp.concatenate([tiles[i], tiles[i + 1]], axis=0 if turned else 1)
        contract = (((1,), (1 if turned else 0,)), ((), ()))
        both = lax.dot_general(left, right, contract, preferred_element_type=f32)
        width = lefts[i].shape[0]
        results += [both[:width, :edge], both[width:, edge:]]
    return results


def fetch(work, vals_ref, held, sems, start, stop):
    def some(k, carry):
        for i in range(group):
            tile = work[jnp.minimum(start + k * group + i, stop - 1)] & 511
            pltpu.make_async_copy(vals_ref.at[tile], held.at[k * group + i], sems.at[k]).start()
        return carry

    lax.fori_loop(0, (stop - start + group - 1) // group, some, 0)


def visit(work, vals_ref, held, sems, table, total, start, stop, turned):
    spare = total.shape[0] - 1

    def some(k, carry):
        slot = k * group
        first = start + slot
        lefts, tiles, places = [], [], []
        for i in range(group):
            code = work[jnp.minimum(first + i, stop - 1)]
            target = (code >> 9) & 511
            source = code >> 18
            lefts.append(table[source if turned else target])
            places.append(jnp.where(first + i < stop, target if turned else source, spare))
        pltpu.make_async_copy(
            vals_ref.at[pl.ds(0, group)], held.at[pl.ds(slot, group)], sems.at[k]
        ).wait()
        for i in range(group):
            tiles.append(held[slot + i])
        for place, product in zip(places, products_of(lefts, tiles, turned)):
            total[place] += product
        return carry

    lax.fori_loop(0, (stop - start + group - 1) // group, some, 0)


def own_kernel(
    dst_ref,
    src_ref,
    count_ref,
    feats_ref,
    vals_ref,
    total_ref,
    work_ref,
    dst,
    src,
    count,
    work,
    near,
    table,
    total,
    held,
    sems,
    tile_sems,
):
    width, nodes = feats_ref.shape
    own = nodes // edge
    tiles = vals_ref.shape[0]
    lists = [
        pltpu.make_async_copy(count_ref, count, sems.at[0]),
        pltpu.make_async_copy(dst_ref, dst, sems.at[1]),
        pltpu.make_async_copy(src_ref, src, sems.at[2]),
    ]
    for copy in lists:
        copy.start()
    features = pltpu.make_async_copy(feats_ref, near, sems.at[3])
    features.start()
    total[...] = jnp.zeros_like(total)
    lists[0].wait()
    live = count[0]
    for copy in lists[1:]:
        copy.wait()

    def sort(t, ends):
        low, high = ends
        source = src[t]
        far = source >= own
        work[jnp.where(far, high, low)] = t + (dst[t] << 9) + (source << 18)
        return jnp.where(far, low, low + 1), jnp.where(far, high - 1, high)

    middle, _ = lax.fori_loop(0, live, sort, (0, live - 1))
    work[tiles] = middle
    work[tiles + 1] = live
    record = pltpu.make_async_copy(work, work_ref, sems.at[4])
    record.start()
    fetch(work, vals_ref, held, tile_sems, 0, middle)
    features.wait()
    for b in range(own):
        table[b] = near[:, b * edge : (b + 1) * edge]

    visit(work, vals_ref, held, tile_sems, table, total, 0, middle, True)
    total_ref[...] = total[0:own]
    record.wait()


def own_tiles(dst, src, count, feats, vals):
    width, nodes = feats.shape
    own = nodes // edge
    tiles = vals.shape[0]
    return pl.pallas_call(
        own_kernel,
        out_shape=(
            jax.ShapeDtypeStruct((own, width, edge), f32),
            jax.ShapeDtypeStruct((tiles + edge,), jnp.int32),
        ),
        in_specs=[hbm] * 5,
        out_specs=(vmem, vmem),
        scratch_shapes=[
            pltpu.SMEM((tiles,), jnp.int32),
            pltpu.SMEM((tiles,), jnp.int32),
            pltpu.SMEM((1,), jnp.int32),
            pltpu.SMEM((tiles + edge,), jnp.int32),
            pltpu.VMEM((width, nodes), bf16),
            pltpu.VMEM((own, width, edge), bf16),
            pltpu.VMEM((own + 1, width, edge), f32),
            pltpu.VMEM((tiles, edge, edge), bf16),
            pltpu.SemaphoreType.DMA((5,)),
            pltpu.SemaphoreType.DMA((tiles // group,)),
        ],
        compiler_params=params(32),
        name="own_tiles",
    )(*far_off(dst, src), count, *far_off(feats, vals))


def far_kernel(work, recv_ref, begun_ref, vals_ref, out_ref, table, total, held, tile_sems):
    own, width, _ = begun_ref.shape
    domains = recv_ref.shape[0]
    peers = out_ref.shape[0]
    tiles = vals_ref.shape[0]
    start, stop = work[tiles], work[tiles + 1]
    fetch(work, vals_ref, held, tile_sems, start, stop)
    lane = lanes(width)
    for g in range(domains // 2):
        table[own + g] = jnp.where(
            lane < edge // 2,
            recv_ref[2 * g, width : 2 * width].astype(f32),
            recv_ref[2 * g + 1, width : 2 * width].astype(f32),
        ).astype(bf16)
    for q in range(domains):
        table[own + domains // 2 + q] = recv_ref[q, 0:width]
    total[0:own] = begun_ref[...]
    visit(work, vals_ref, held, tile_sems, table, total, start, stop, True)
    per = own // peers
    for b in range(own):
        col = (b % per) * edge
        out_ref[b // per, :, col : col + edge] = total[b].astype(bf16)


def far_tiles(work, recv, begun, vals, peers):
    own, width, _ = begun.shape
    domains = recv.shape[0]
    nodes = own * edge
    tiles = vals.shape[0]
    return pl.pallas_call(
        far_kernel,
        out_shape=jax.ShapeDtypeStruct((peers, width, nodes // peers), bf16),
        in_specs=[smem, vmem, vmem, hbm],
        out_specs=vmem,
        scratch_shapes=[
            pltpu.VMEM((own + domains // 2 + domains, width, edge), bf16),
            pltpu.VMEM((own + 1, width, edge), f32),
            pltpu.VMEM((tiles, edge, edge), bf16),
            pltpu.SemaphoreType.DMA((tiles // group,)),
        ],
        compiler_params=params(32),
        name="far_tiles",
    )(work, recv, begun, *far_off(vals))


def fill_blocks(near_ref, blocks):
    own = blocks.shape[0]
    per = own // near_ref.shape[0]
    for b in range(own):
        col = (b % per) * edge
        blocks[b] = near_ref[b // per, :, col : col + edge]


def away_kernel(work, near_ref, vals_ref, out_ref, blocks, total, held, tile_sems):
    peers, width, _ = near_ref.shape
    own = blocks.shape[0]
    share = own // peers * edge
    domains = out_ref.shape[0]
    far = own + domains // 2
    tiles = vals_ref.shape[0]
    start, stop = work[tiles], work[tiles + 1]
    fetch(work, vals_ref, held, tile_sems, start, stop)
    fill_blocks(near_ref, blocks)
    total[...] = jnp.zeros_like(total)

    def summed(place):
        start = share + place * edge
        return jnp.sum(near_ref[:, :, start : start + edge].astype(f32), axis=0)

    grad_self = summed(0).astype(bf16)
    grad_neigh = summed(1).astype(bf16)
    grad_bias = column_block(jnp.sum(summed(2), axis=1, keepdims=True))
    grad_bias = pltpu.roll(grad_bias, edge // 2, 1)
    visit(work, vals_ref, held, tile_sems, blocks, total, start, stop, False)
    lane = lanes(width)
    for g in range(domains // 2):
        here = total[own + g]
        for odd in range(2):
            q = 2 * g + odd
            mine = pltpu.roll(here, edge // 2, 1) if odd else here
            out_ref[q, 0:width] = total[far + q].astype(bf16)
            out_ref[q, width : 2 * width] = jnp.where(lane < edge // 2, mine, grad_bias).astype(bf16)
            out_ref[q, 2 * width : 3 * width] = grad_self
            out_ref[q, 3 * width : 4 * width] = grad_neigh


def away(work, near, vals, domains, nodes):
    _, width, _ = near.shape
    tiles = vals.shape[0]
    own = nodes // edge
    return pl.pallas_call(
        away_kernel,
        out_shape=jax.ShapeDtypeStruct((domains, 4 * width, edge), bf16),
        in_specs=[smem, vmem, hbm],
        out_specs=vmem,
        scratch_shapes=[
            pltpu.VMEM((own, width, edge), bf16),
            pltpu.VMEM((own + domains // 2 + domains + 1, width, edge), f32),
            pltpu.VMEM((tiles, edge, edge), bf16),
            pltpu.SemaphoreType.DMA((tiles // group,)),
        ],
        compiler_params=params(32),
        name="away",
    )(work, near, *far_off(vals))


def home_kernel(work, near_ref, vals_ref, out_ref, blocks, total, held, tile_sems):
    own = blocks.shape[0]
    tiles = vals_ref.shape[0]
    stop = work[tiles]
    fetch(work, vals_ref, held, tile_sems, 0, stop)
    fill_blocks(near_ref, blocks)
    total[...] = jnp.zeros_like(total)
    visit(work, vals_ref, held, tile_sems, blocks, total, 0, stop, False)
    for b in range(own):
        out_ref[:, b * edge : (b + 1) * edge] = total[b]


def home(work, near, vals, nodes):
    _, width, _ = near.shape
    tiles = vals.shape[0]
    own = nodes // edge
    return pl.pallas_call(
        home_kernel,
        out_shape=jax.ShapeDtypeStruct((width, nodes), f32),
        in_specs=[smem, vmem, hbm],
        out_specs=vmem,
        scratch_shapes=[
            pltpu.VMEM((own, width, edge), bf16),
            pltpu.VMEM((own + 1, width, edge), f32),
            pltpu.VMEM((tiles, edge, edge), bf16),
            pltpu.SemaphoreType.DMA((tiles // group,)),
        ],
        compiler_params=params(32),
        name="home",
    )(work, near, *far_off(vals))


def layer_kernel(agg_ref, *rest):
    peers, width, share = agg_ref.shape
    rows = peers * width
    parts, near_ref, lates = rest[:peers], rest[peers], rest[peers + 1 : 2 * peers + 1]
    feats_all, cotangent_all, self_all, neigh_all, bias_all, act, back = rest[2 * peers + 1 :]
    here = lax.axis_index("feat")
    for k, part in enumerate(parts):
        peer = here ^ k
        feats_all[peer] = part[:, 0:share]
        cotangent_all[peer] = part[:, share : 2 * share]
        self_all[peer] = part[:, 2 * share : 2 * share + edge]
        neigh_all[peer] = part[:, 2 * share + edge : 2 * share + 2 * edge]
        bias_all[peer] = part[:, 2 * share + 2 * edge : 2 * share + 3 * edge]
    feats = feats_all[...].reshape(rows, share)
    cotangent = cotangent_all[...].reshape(rows, share)
    w_self = self_all[...].reshape(rows, edge)
    w_neigh = neigh_all[...].reshape(rows, edge)
    bias = jnp.sum(bias_all[...].reshape(rows, edge).astype(f32), axis=1, keepdims=True)
    aggregate = agg_ref[...].reshape(rows, share)
    first = (((0,), (0,)), ((), ()))
    last = (((1,), (1,)), ((), ()))
    linear = lax.dot_general(w_self, feats, first, preferred_element_type=f32)
    linear = linear + lax.dot_general(w_neigh, aggregate, first, preferred_element_type=f32)
    linear = linear + bias
    logistic = jax.nn.sigmoid(linear)
    act[...] = (linear * logistic).astype(bf16).reshape(peers, width, share)
    slope = logistic * (1.0 + linear * (1.0 - logistic))
    grad = (cotangent.astype(f32) * slope).astype(bf16)
    near_ref[:, :, 0:share] = (
        jnp.dot(w_neigh, grad, preferred_element_type=f32).astype(bf16).reshape(peers, width, share)
    )
    back[...] = (
        jnp.dot(w_self, grad, preferred_element_type=f32).astype(bf16).reshape(peers, width, share)
    )
    grad_self = lax.dot_general(feats, grad, last, preferred_element_type=f32)
    grad_neigh = lax.dot_general(aggregate, grad, last, preferred_element_type=f32)
    grad_bias = column_block(jnp.sum(grad.astype(f32), axis=1, keepdims=True)).astype(bf16)
    for place, piece in enumerate((grad_self.astype(bf16), grad_neigh.astype(bf16), grad_bias)):
        start = share + place * edge
        near_ref[:, :, start : start + edge] = piece.reshape(peers, width, edge)
    for k, late in enumerate(lates):
        peer = here ^ k
        late[:, 0:share] = act[peer]
        late[:, share : 2 * share] = back[peer]


def layer(agg, parts):
    peers, width, share = agg.shape
    return pl.pallas_call(
        layer_kernel,
        out_shape=(jax.ShapeDtypeStruct((peers, width, share + 3 * edge), bf16),)
        + (jax.ShapeDtypeStruct((width, 2 * share), bf16),) * peers,
        in_specs=[vmem] * (1 + peers),
        out_specs=(vmem,) * (1 + peers),
        scratch_shapes=[
            pltpu.VMEM((peers, width, share), bf16),
            pltpu.VMEM((peers, width, share), bf16),
            pltpu.VMEM((peers, width, edge), bf16),
            pltpu.VMEM((peers, width, edge), bf16),
            pltpu.VMEM((peers, width, edge), bf16),
            pltpu.VMEM((peers, width, share), bf16),
            pltpu.VMEM((peers, width, share), bf16),
        ],
        compiler_params=params(32),
        name="layer",
    )(agg, *parts)


def settle_kernel(scale, home_ref, hot_ref, recv_ref, base_ref, *rest):
    width, nodes = base_ref.shape
    lates, rest = rest[:-8], rest[-8:]
    act_ref, feats_ref, self_ref, neigh_ref, bias_ref, marked, hots, back = rest
    domains = recv_ref.shape[0]
    peers = len(lates)
    share = nodes // peers
    count = nodes // span
    pairs = domains // 2
    here = lax.axis_index("feat")
    for k, late in enumerate(lates):
        peer = here ^ k
        act_ref[:, pl.ds(pl.multiple_of(peer * share, share), share)] = late[:, 0:share]
        back[:, pl.ds(pl.multiple_of(peer * share, share), share)] = late[:, share : 2 * share]
    lane = lanes(width)

    def over(start):
        return jnp.sum(recv_ref[:, start : start + width].astype(f32), axis=0)

    hub = over(0)
    self_ref[...] = over(2 * width) * scale
    neigh_ref[...] = over(3 * width) * scale
    tail = jnp.where(lane >= edge // 2, over(width), 0.0)
    column = jnp.broadcast_to(jnp.sum(tail, axis=1, keepdims=True) * scale, (width, edge))
    row = lax.broadcasted_iota(jnp.int32, (width, edge), 0)
    bias_ref[...] = jnp.sum(jnp.where(row == lane, column, 0.0), axis=0)[:width]
    hub_pieces = split(hub, 3)
    for g in range(pairs + 3):
        if g < pairs:
            first = recv_ref[2 * g, width : 2 * width].astype(f32)
            second = pltpu.roll(recv_ref[2 * g + 1, width : 2 * width].astype(f32), edge // 2, 1)
            value = jnp.where(lane < edge // 2, first, second)
        else:
            value = hub_pieces[g - pairs].astype(f32)
        at = min(g, pairs)
        where = jnp.broadcast_to(home_ref[at : at + 1, :], (width, edge))
        hots[:, g * edge : (g + 1) * edge] = hot_ref[at]
        for b in range(count):
            marked[b * width : (b + 1) * width, g * edge : (g + 1) * edge] = jnp.where(
                where == b, value, 0.0
            ).astype(bf16)
    placed = lax.dot_general(
        marked[...], hots[...], (((1,), (1,)), ((), ())), preferred_element_type=f32
    )
    for b in range(count):
        cols = slice(b * span, (b + 1) * span)
        feats_ref[:, cols] = (
            back[:, cols].astype(f32) + base_ref[:, cols] + placed[b * width : (b + 1) * width]
        ).astype(bf16)


def settle(homes, hot, recv, base, lates, scale):
    width, nodes = base.shape
    domains = recv.shape[0]
    terms = (domains // 2 + 3) * edge
    return pl.pallas_call(
        functools.partial(settle_kernel, scale),
        out_shape=(
            jax.ShapeDtypeStruct((width, nodes), bf16),
            jax.ShapeDtypeStruct((width, nodes), bf16),
            jax.ShapeDtypeStruct((width, edge), f32),
            jax.ShapeDtypeStruct((width, edge), f32),
            jax.ShapeDtypeStruct((width,), f32),
        ),
        in_specs=[vmem] * (4 + len(lates)),
        out_specs=(vmem,) * 5,
        scratch_shapes=[
            pltpu.VMEM((nodes // span * width, terms), bf16),
            pltpu.VMEM((span, terms), bf16),
            pltpu.VMEM((width, nodes), bf16),
        ],
        compiler_params=params(32),
        name="settle",
    )(homes, hot, recv, base, *lates)


def swap(values, axis):
    return lax.all_to_all(values, axis, split_axis=0, concat_axis=0, tiled=True)


def trade(parts, axis):
    peers = len(parts)
    return [
        part if k == 0 else lax.ppermute(part, axis, [(i, i ^ k) for i in range(peers)])
        for k, part in enumerate(parts)
    ]


def local(
    feats,
    tile_vals,
    tile_dst,
    tile_src,
    tile_count,
    send_rows,
    hub_ids,
    w_self,
    w_neigh,
    bias,
    cotangent,
):
    nodes = feats.shape[1]
    domains = lax.axis_size("dom")
    peers = lax.axis_size("feat")
    picked, hot, homes = pick(send_rows[0], hub_ids, feats)
    picked, bias = lax.optimization_barrier((picked, bias))
    recv = swap(picked, "dom")
    parts = trade(deal(feats, cotangent, w_self, w_neigh, bias, peers), "feat")
    begun, work = own_tiles(tile_dst, tile_src, tile_count, feats, tile_vals)
    recv, parts = lax.optimization_barrier((recv, parts))
    agg = swap(far_tiles(work, recv, begun, tile_vals, peers), "feat")
    near, *lates = layer(agg, parts)
    near = swap(near, "feat")
    back = away(work, near, tile_vals, domains, nodes)
    back, lates = lax.optimization_barrier((back, lates))
    back = swap(back, "dom")
    lates = trade(lates, "feat")
    base = home(work, near, tile_vals, nodes)
    scale = 1.0 / math.sqrt(nodes * domains)
    return settle(homes, hot, back, base, lates, scale)


def solution(mesh):
    placed = (
        P("feat", "dom"),
        P("dom", None, None),
        P("dom"),
        P("dom"),
        P("dom"),
        P("dom", None, None),
        P("dom"),
        P("feat", None),
        P("feat", None),
        P("feat"),
        P("feat", "dom"),
    )
    return jax.shard_map(
        local,
        mesh=mesh,
        in_specs=placed,
        out_specs=(P("feat", "dom"), P("feat", "dom"), P("feat", None), P("feat", None), P("feat")),
        check_vma=False,
    )
```

time: 119 us -> 94 us (0.79)
  blocking collectives: 49.5 us -> 20.9 us
  starting transfers between devices: 19.1 us -> 41.2 us
  local copies, waits for them, and re-layouts: 8.07 us -> 0 us
  waiting for transfers between devices: 15.9 us -> 8.87 us
  Pallas kernels: 22.9 us -> 21.3 us
  other arithmetic: 1.29 us -> 0 us
    all_to_all x3 -> x2, blocking collectives: 49.5 us -> 20.9 us  [swap(): return lax.all_to_all(values, axis, split_axis=0, concat_axis=0, tiled=True)]
    ppermute x0 -> x14, starting transfers between devices: none -> 16.4 us  [trade(): lax.ppermute(part, axis, [(i, i ^ k) for i in range(peers)])]
    all_to_all x3 -> x2, waiting for transfers between devices: 15.9 us -> 5.6 us  [swap(): return lax.all_to_all(values, axis, split_axis=0, concat_axis=0, tiled=True)]
    unnamed x20 -> x0, local copies, waits for them, and re-layouts: 6.54 us -> none
    all_to_all x3 -> x2, starting transfers between devices: 19.1 us -> 24.8 us  [swap(): return lax.all_to_all(values, axis, split_axis=0, concat_axis=0, tiled=True)]
    pallas_call x1, Pallas kernels: 5.48 us -> 1.79 us  [settle(): pl.pallas_call(functools.partial(settle_kernel, scale), out_shape=(jax.Sh...]
    ppermute x0 -> x14, waiting for transfers between devices: none -> 3.28 us  [trade(): lax.ppermute(part, axis, [(i, i ^ k) for i in range(peers)])]
    pallas_call x4 -> x6, Pallas kernels: 15.9 us -> 18.6 us  [the longest x1 4.29 us: own_tiles(): pl.pallas_call(own_kernel, out_shape=(jax.ShapeDtypeStruct((own, width, e...]
  transfers between devices with their start and end apart: 3 -> 16, of which waited for: 3 -> 5; matrix products, arithmetic and copies ran while one was open for 1% -> 0% of each run, Pallas kernels for 9% -> 9%
where the time goes in v2:
time: 94 us; the launch traced here: 93.7 us
  starting transfers between devices  41.2 us (44%)
  Pallas kernels  21.3 us (23%)
  blocking collectives  20.9 us (22%)
  waiting for transfers between devices  8.87 us (9%)
  between operations  1.42 us (2%)
    all_to_all x2, starting transfers between devices, swap(): return lax.all_to_all(values, axis, split_axis=0, concat_axis=0, tiled=True)  24.8 us
    all_to_all x2, blocking collectives, swap(): return lax.all_to_all(values, axis, split_axis=0, concat_axis=0, tiled=True)  20.9 us
    ppermute x14, starting transfers between devices, trade(): lax.ppermute(part, axis, [(i, i ^ k) for i in range(peers)])  16.4 us
    all_to_all x2, waiting for transfers between devices, swap(): return lax.all_to_all(values, axis, split_axis=0, concat_axis=0, tiled=True)  5.6 us
    pallas_call x1, Pallas kernels, own_tiles(): pl.pallas_call(own_kernel, out_shape=(jax.ShapeDtypeStruct((own, width, e...  4.29 us
    pallas_call x1, Pallas kernels, pick(): pl.pallas_call(pick_kernel, out_shape=(jax.ShapeDtypeStruct((domains, 2 *...  3.77 us
    pallas_call x1, Pallas kernels, away(): pl.pallas_call(away_kernel, out_shape=jax.ShapeDtypeStruct((domains, 4 *...  3.75 us
    ppermute x14, waiting for transfers between devices, trade(): lax.ppermute(part, axis, [(i, i ^ k) for i in range(peers)])  3.28 us
  transfers between devices with their start and end apart: 16, of which 5 were waited for; matrix products, arithmetic and copies ran while one was open for 0% of the time, Pallas kernels for 9%

profile of v2, /device:TPU:32, one launch (start us, length us, event | category | flops | bytes accessed | tf_op | source)
XLA Modules:
  0.0 93.7 jit_solution(17709640450615532352)
XLA Ops:
  0.6 3.8 %pick.1 = (bf16[32,32,128]{2,1,0:T(8,128)(2,1)}, bf16[17,256,128]{2,1,0:T(8,128)(2,1)S(1)}, s32[17,128]{1,0:T(8,128)S(1)}) custom-call(s32[32,64]{1,0:T(8,128)} %bitcast.1, s32[128]{0:T(128)} %hub_ref.1, bf16[16,8192]{1,0:T(8,128)(2,1)} %feats_ref.5), custom_call_target="tpu_custom_call" | custom-call | tf_op jit(solution)/shard_map/pick/pallas_call | solution.py:108
  4.4 11.4 %all-to-all-start = ((bf16[32,32,128]{2,1,0:T(8,128)(2,1)}), bf16[32,32,128]{2,1,0:T(8,128)(2,1)S(1)}, u32[]{:S(2)}, u32[]{:S(2)}) async-start(bf16[32,32,128]{2,1,0:T(8,128)(2,1)} %get-tuple-element.51), calls=%async_computation | async-start | bytes 524288 | tf_op jit(solution)/shard_map/all_to_all | solution.py:609
  15.8 1.2 %deal.1 = (bf16[16,2432]{1,0:T(8,128)(2,1)S(1)}, bf16[16,2432]{1,0:T(8,128)(2,1)S(1)}, bf16[16,2432]{1,0:T(8,128)(2,1)S(1)}, bf16[16,2432]{1,0:T(8,128)(2,1)S(1)...) custom-call(bf16[16,8192]{1,0:T(8,128)(2,1)} %feats_ref.5, ...), custom_call_target="tpu_custom_call" | custom-call | tf_op jit(solution)/shard_map/deal/pallas_call | solution.py:175
  17.0 0.1 collective-permute-start
  17.1 1.6 %collective-permute-start.1 = (bf16[16,2432]{1,0:T(8,128)(2,1)S(1)}, bf16[16,2432]{1,0:T(8,128)(2,1)S(1)}, u32[]{:S(2)}, u32[]{:S(2)}) collective-permute-start(bf16[16,2432]{1,0:T(8,128)(2,1)S(1)} %get-tuple-element.55), channel_id=1, source_target_pairs={{0,2},{1,3},{2,0},{3,1},{4,6},{5,7},{6,4},{7,5},{8,10},{9,11},{10,... | collective-permute-start | bytes 233480 | tf_op jit(solution)/shard_map/ppermute | solution.py:615
  18.7 0.3 collective-permute-start.2
  19.0 3.0 %collective-permute-start.3 = (bf16[16,2432]{1,0:T(8,128)(2,1)S(1)}, bf16[16,2432]{1,0:T(8,128)(2,1)S(1)}, u32[]{:S(2)}, u32[]{:S(2)}) collective-permute-start(bf16[16,2432]{1,0:T(8,128)(2,1)S(1)} %get-tuple-element.57), channel_id=1, source_target_pairs={{0,4},{1,5},{2,6},{3,7},{4,0},{5,1},{6,2},{7,3},{8,12},{9,13},{10,... | collective-permute-start | bytes 233480 | tf_op jit(solution)/shard_map/ppermute | solution.py:615
  22.0 0.2 collective-permute-start.4
  22.2 0.0 collective-permute-done.rest_1_
  22.2 2.8 %collective-permute-start.5 = (bf16[16,2432]{1,0:T(8,128)(2,1)S(1)}, bf16[16,2432]{1,0:T(8,128)(2,1)S(1)}, u32[]{:S(2)}, u32[]{:S(2)}) collective-permute-start(bf16[16,2432]{1,0:T(8,128)(2,1)S(1)} %get-tuple-element.59), channel_id=1, source_target_pairs={{0,6},{1,7},{2,4},{3,5},{4,2},{5,3},{6,0},{7,1},{8,14},{9,15},{10,... | collective-permute-start | bytes 233480 | tf_op jit(solution)/shard_map/ppermute | solution.py:615
  25.0 0.0 collective-permute-done.1.rest_2_
  25.0 0.2 collective-permute-start.6
  25.9 4.3 %own_tiles.1 = (f32[64,16,128]{2,1,0:T(8,128)S(1)}, s32[448]{0:T(512)S(1)}) custom-call(s32[320]{0:T(512)} %dst_ref.1, s32[320]{0:T(512)} %src_ref.1, s32[1]{0:T(128)S(6)} %copy.16.count_ref, bf16[16,8192]{1,0:T(8,128)(2,1)} %feats_ref.5, bf16[320,128,128]{2,1,0:T(8,128)(2,1)} %vals_ref.7), custom_call_target="tpu_custom_call" | custom-call | tf_op jit(solution)/shard_map/own_tiles/pallas_call | solution.py:301
  30.2 0.0 collective-permute-done.2.rest_3_
  30.2 0.0 collective-permute-done.3.rest_4_
  30.2 0.0 collective-permute-done.4.rest_5_
  30.2 0.6 collective-permute-done.5.rest_6_
  30.8 1.6 %collective-permute-done.6.rest_7_ = bf16[16,2432]{1,0:T(8,128)(2,1)S(1)} collective-permute-done((bf16[16,2432]{1,0:T(8,128)(2,1)S(1)}, bf16[16,2432]{1,0:T(8,128)(2,1)S(1)}, u32[]{:S(2)}, u32[]{:S(2)}) %collective-permute-start.6) | collective-permute-done | bytes 77856 | tf_op jit(solution)/shard_map/ppermute | solution.py:615
  32.4 0.0 all-to-all-done.recv_ref
  32.4 3.0 %far_tiles.1 = bf16[8,16,1024]{2,1,0:T(8,128)(2,1)S(1)} custom-call(s32[448]{0:T(512)S(1)} %get-tuple-element.49.work, bf16[32,32,128]{2,1,0:T(8,128)(2,1)S(1)} %all-to-all-done.recv_ref, f32[64,16,128]{2,1,0:T(8,128)S(1)} %get-tuple-element.62.begun_ref, bf16[320,128,128]{2,1,0:T(8,128)(2,1)} %vals_ref.7), custom_call_target="tpu_custom_call" | custom-call | tf_op jit(solution)/shard_map/far_tiles/pallas_call | solution.py:355
  35.4 9.9 %all_to_all.20.agg_ref = bf16[8,16,1024]{2,1,0:T(8,128)(2,1)S(1)} all-to-all(bf16[8,16,1024]{2,1,0:T(8,128)(2,1)S(1)} %far_tiles.1), channel_id=1, replica_groups=mesh['dom'=32,'feat'=8] {'feat'}, dimensions={0} | all-to-all | bytes 524288 | tf_op jit(solution)/shard_map/all_to_all | solution.py:609
  45.4 0.9 layer.1
  46.3 11.0 %all_to_all.21.near_ref = bf16[8,16,1408]{2,1,0:T(8,128)(2,1)S(1)} all-to-all(bf16[8,16,1408]{2,1,0:T(8,128)(2,1)S(1)} %get-tuple-element.71), channel_id=1, replica_groups=mesh['dom'=32,'feat'=8] {'feat'}, dimensions={0} | all-to-all | bytes 720896 | tf_op jit(solution)/shard_map/all_to_all | solution.py:609
  57.2 3.8 %away.1 = bf16[32,64,128]{2,1,0:T(8,128)(2,1)} custom-call(s32[448]{0:T(512)S(1)} %get-tuple-element.49.work, bf16[8,16,1408]{2,1,0:T(8,128)(2,1)S(1)} %all_to_all.21.near_ref, bf16[320,128,128]{2,1,0:T(8,128)(2,1)} %vals_ref.7), custom_call_target="tpu_custom_call" | custom-call | tf_op jit(solution)/shard_map/away/pallas_call | solution.py:416
  61.0 13.4 %all-to-all-start.3 = ((bf16[32,64,128]{2,1,0:T(8,128)(2,1)}), bf16[32,64,128]{2,1,0:T(8,128)(2,1)S(1)}, u32[]{:S(2)}, u32[]{:S(2)}) async-start(bf16[32,64,128]{2,1,0:T(8,128)(2,1)} %away.1), calls=%async_computation.3 | async-start | bytes 1048576 | tf_op jit(solution)/shard_map/all_to_all | solution.py:609
  74.4 0.1 collective-permute-start.7
  74.5 0.7 collective-permute-start.8
  75.2 1.2 %collective-permute-start.9 = (bf16[16,2048]{1,0:T(8,128)(2,1)S(1)}, bf16[16,2048]{1,0:T(8,128)(2,1)S(1)}, u32[]{:S(2)}, u32[]{:S(2)}) collective-permute-start(bf16[16,2048]{1,0:T(8,128)(2,1)S(1)} %get-tuple-element.84), channel_id=1, source_target_pairs={{0,3},{1,2},{2,1},{3,0},{4,7},{5,6},{6,5},{7,4},{8,11},{9,10},{10,... | collective-permute-start | bytes 196616 | tf_op jit(solution)/shard_map/ppermute | solution.py:615
  76.4 0.9 collective-permute-start.10
  77.3 2.3 %collective-permute-start.11 = (bf16[16,2048]{1,0:T(8,128)(2,1)S(1)}, bf16[16,2048]{1,0:T(8,128)(2,1)S(1)}, u32[]{:S(2)}, u32[]{:S(2)}) collective-permute-start(bf16[16,2048]{1,0:T(8,128)(2,1)S(1)} %get-tuple-element.86), channel_id=1, source_target_pairs={{0,5},{1,4},{2,7},{3,6},{4,1},{5,0},{6,3},{7,2},{8,13},{9,12},{10,... | collective-permute-start | bytes 196616 | tf_op jit(solution)/shard_map/ppermute | solution.py:615
  79.6 0.0 collective-permute-done.7.rest_1_
  79.6 1.2 %collective-permute-start.12 = (bf16[16,2048]{1,0:T(8,128)(2,1)S(1)}, bf16[16,2048]{1,0:T(8,128)(2,1)S(1)}, u32[]{:S(2)}, u32[]{:S(2)}) collective-permute-start(bf16[16,2048]{1,0:T(8,128)(2,1)S(1)} %get-tuple-element.87), channel_id=1, source_target_pairs={{0,6},{1,7},{2,4},{3,5},{4,2},{5,3},{6,0},{7,1},{8,14},{9,15},{10,... | collective-permute-start | bytes 196616 | tf_op jit(solution)/shard_map/ppermute | solution.py:615
  80.8 0.0 collective-permute-done.8.rest_2_
  80.8 1.8 %collective-permute-start.13 = (bf16[16,2048]{1,0:T(8,128)(2,1)S(1)}, bf16[16,2048]{1,0:T(8,128)(2,1)S(1)}, u32[]{:S(2)}, u32[]{:S(2)}) collective-permute-start(bf16[16,2048]{1,0:T(8,128)(2,1)S(1)} %get-tuple-element.88), channel_id=1, source_target_pairs={{0,7},{1,6},{2,5},{3,4},{4,3},{5,2},{6,1},{7,0},{8,15},{9,14},{10,... | collective-permute-start | bytes 196616 | tf_op jit(solution)/shard_map/ppermute | solution.py:615
  82.6 2.6 %home.1.base_ref = f32[16,8192]{1,0:T(8,128)S(1)} custom-call(s32[448]{0:T(512)S(1)} %get-tuple-element.49.work, bf16[8,16,1408]{2,1,0:T(8,128)(2,1)S(1)} %all_to_all.21.near_ref, bf16[320,128,128]{2,1,0:T(8,128)(2,1)} %vals_ref.7), custom_call_target="tpu_custom_call" | custom-call | tf_op jit(solution)/shard_map/home/pallas_call | solution.py:448
  85.2 0.0 collective-permute-done.9.rest_3_
  85.3 0.0 collective-permute-done.10.rest_4_
  85.3 0.0 collective-permute-done.11.rest_5_
  85.3 0.4 collective-permute-done.12.rest_6_
  85.6 0.7 collective-permute-done.13.rest_7_
  86.3 5.6 %all-to-all-done.3.recv_ref = bf16[32,64,128]{2,1,0:T(8,128)(2,1)S(1)} async-done(((bf16[32,64,128]{2,1,0:T(8,128)(2,1)}), bf16[32,64,128]{2,1,0:T(8,128)(2,1)S(1)}, u32[]{:S(2)}, u32[]{:S(2)}) %all-to-all-start.3) | async-done | bytes 524320 | tf_op jit(solution)/shard_map/all_to_all | solution.py:609
  91.9 1.8 %settle.1 = (bf16[16,8192]{1,0:T(8,128)(2,1)}, bf16[16,8192]{1,0:T(8,128)(2,1)}, f32[16,128]{1,0:T(8,128)}, f32[16,128]{1,0:T(8,128)}, f32[16]{0:T(128)}) custom-call(s32[17,128]{1,0:T(8,128)S(1)} %get-tuple-element.47.home_ref, bf16[17,256,128]{2,1,0:T(8,128)(2,1)S(1)} %get-tuple-element.48.hot_ref, bf16[32,64,128]{2,1,0:T(8,128)(2,1)S(1)} %all-to-all-done.3.recv_ref, ...), custom_call_target="tpu_custom_call" | custom-call | tf_op jit(solution)/shard_map/settle/pallas_call | solution.py:587
Async XLA Ops:
  4.4 28.0 %all-to-all-start = ((bf16[32,32,128]{2,1,0:T(8,128)(2,1)}), bf16[32,32,128]{2,1,0:T(8,128)(2,1)S(1)}, u32[]{:S(2)}, u32[]{:S(2)}) async-start(bf16[32,32,128]{2,1,0:T(8,128)(2,1)} %get-tuple-element.51), calls=%async_computation | async-start | bytes 524288 | tf_op jit(solution)/shard_map/all_to_all | solution.py:609
  17.0 5.2 %collective-permute-start = (bf16[16,2432]{1,0:T(8,128)(2,1)S(1)}, bf16[16,2432]{1,0:T(8,128)(2,1)S(1)}, u32[]{:S(2)}, u32[]{:S(2)}) collective-permute-start(bf16[16,2432]{1,0:T(8,128)(2,1)S(1)} %get-tuple-element.54), channel_id=1, source_target_pairs={{0,1},{1,0},{2,3},{3,2},{4,5},{5,4},{6,7},{7,6},{8,9},{9,8},{10,11... | collective-permute-start | bytes 233480 | tf_op jit(solution)/shard_map/ppermute | solution.py:615
  17.1 7.8 %collective-permute-start.1 = (bf16[16,2432]{1,0:T(8,128)(2,1)S(1)}, bf16[16,2432]{1,0:T(8,128)(2,1)S(1)}, u32[]{:S(2)}, u32[]{:S(2)}) collective-permute-start(bf16[16,2432]{1,0:T(8,128)(2,1)S(1)} %get-tuple-element.55), channel_id=1, source_target_pairs={{0,2},{1,3},{2,0},{3,1},{4,6},{5,7},{6,4},{7,5},{8,10},{9,11},{10,... | collective-permute-start | bytes 233480 | tf_op jit(solution)/shard_map/ppermute | solution.py:615
  18.7 11.5 %collective-permute-start.2 = (bf16[16,2432]{1,0:T(8,128)(2,1)S(1)}, bf16[16,2432]{1,0:T(8,128)(2,1)S(1)}, u32[]{:S(2)}, u32[]{:S(2)}) collective-permute-start(bf16[16,2432]{1,0:T(8,128)(2,1)S(1)} %get-tuple-element.56), channel_id=1, source_target_pairs={{0,3},{1,2},{2,1},{3,0},{4,7},{5,6},{6,5},{7,4},{8,11},{9,10},{10,... | collective-permute-start | bytes 233480 | tf_op jit(solution)/shard_map/ppermute | solution.py:615
  19.0 11.2 %collective-permute-start.3 = (bf16[16,2432]{1,0:T(8,128)(2,1)S(1)}, bf16[16,2432]{1,0:T(8,128)(2,1)S(1)}, u32[]{:S(2)}, u32[]{:S(2)}) collective-permute-start(bf16[16,2432]{1,0:T(8,128)(2,1)S(1)} %get-tuple-element.57), channel_id=1, source_target_pairs={{0,4},{1,5},{2,6},{3,7},{4,0},{5,1},{6,2},{7,3},{8,12},{9,13},{10,... | collective-permute-start | bytes 233480 | tf_op jit(solution)/shard_map/ppermute | solution.py:615
  22.0 8.2 %collective-permute-start.4 = (bf16[16,2432]{1,0:T(8,128)(2,1)S(1)}, bf16[16,2432]{1,0:T(8,128)(2,1)S(1)}, u32[]{:S(2)}, u32[]{:S(2)}) collective-permute-start(bf16[16,2432]{1,0:T(8,128)(2,1)S(1)} %get-tuple-element.58), channel_id=1, source_target_pairs={{0,5},{1,4},{2,7},{3,6},{4,1},{5,0},{6,3},{7,2},{8,13},{9,12},{10,... | collective-permute-start | bytes 233480 | tf_op jit(solution)/shard_map/ppermute | solution.py:615
  22.2 8.6 %collective-permute-start.5 = (bf16[16,2432]{1,0:T(8,128)(2,1)S(1)}, bf16[16,2432]{1,0:T(8,128)(2,1)S(1)}, u32[]{:S(2)}, u32[]{:S(2)}) collective-permute-start(bf16[16,2432]{1,0:T(8,128)(2,1)S(1)} %get-tuple-element.59), channel_id=1, source_target_pairs={{0,6},{1,7},{2,4},{3,5},{4,2},{5,3},{6,0},{7,1},{8,14},{9,15},{10,... | collective-permute-start | bytes 233480 | tf_op jit(solution)/shard_map/ppermute | solution.py:615
  25.0 7.4 %collective-permute-start.6 = (bf16[16,2432]{1,0:T(8,128)(2,1)S(1)}, bf16[16,2432]{1,0:T(8,128)(2,1)S(1)}, u32[]{:S(2)}, u32[]{:S(2)}) collective-permute-start(bf16[16,2432]{1,0:T(8,128)(2,1)S(1)} %get-tuple-element.60), channel_id=1, source_target_pairs={{0,7},{1,6},{2,5},{3,4},{4,3},{5,2},{6,1},{7,0},{8,15},{9,14},{10,... | collective-permute-start | bytes 233480 | tf_op jit(solution)/shard_map/ppermute | solution.py:615
  61.0 30.9 %all-to-all-start.3 = ((bf16[32,64,128]{2,1,0:T(8,128)(2,1)}), bf16[32,64,128]{2,1,0:T(8,128)(2,1)S(1)}, u32[]{:S(2)}, u32[]{:S(2)}) async-start(bf16[32,64,128]{2,1,0:T(8,128)(2,1)} %away.1), calls=%async_computation.3 | async-start | bytes 1048576 | tf_op jit(solution)/shard_map/all_to_all | solution.py:609
  74.4 5.2 %collective-permute-start.7 = (bf16[16,2048]{1,0:T(8,128)(2,1)S(1)}, bf16[16,2048]{1,0:T(8,128)(2,1)S(1)}, u32[]{:S(2)}, u32[]{:S(2)}) collective-permute-start(bf16[16,2048]{1,0:T(8,128)(2,1)S(1)} %get-tuple-element.82), channel_id=1, source_target_pairs={{0,1},{1,0},{2,3},{3,2},{4,5},{5,4},{6,7},{7,6},{8,9},{9,8},{10,11... | collective-permute-start | bytes 196616 | tf_op jit(solution)/shard_map/ppermute | solution.py:615
  74.5 6.3 %collective-permute-start.8 = (bf16[16,2048]{1,0:T(8,128)(2,1)S(1)}, bf16[16,2048]{1,0:T(8,128)(2,1)S(1)}, u32[]{:S(2)}, u32[]{:S(2)}) collective-permute-start(bf16[16,2048]{1,0:T(8,128)(2,1)S(1)} %get-tuple-element.83), channel_id=1, source_target_pairs={{0,2},{1,3},{2,0},{3,1},{4,6},{5,7},{6,4},{7,5},{8,10},{9,11},{10,... | collective-permute-start | bytes 196616 | tf_op jit(solution)/shard_map/ppermute | solution.py:615
  75.2 10.0 %collective-permute-start.9 = (bf16[16,2048]{1,0:T(8,128)(2,1)S(1)}, bf16[16,2048]{1,0:T(8,128)(2,1)S(1)}, u32[]{:S(2)}, u32[]{:S(2)}) collective-permute-start(bf16[16,2048]{1,0:T(8,128)(2,1)S(1)} %get-tuple-element.84), channel_id=1, source_target_pairs={{0,3},{1,2},{2,1},{3,0},{4,7},{5,6},{6,5},{7,4},{8,11},{9,10},{10,... | collective-permute-start | bytes 196616 | tf_op jit(solution)/shard_map/ppermute | solution.py:615
  76.4 8.8 %collective-permute-start.10 = (bf16[16,2048]{1,0:T(8,128)(2,1)S(1)}, bf16[16,2048]{1,0:T(8,128)(2,1)S(1)}, u32[]{:S(2)}, u32[]{:S(2)}) collective-permute-start(bf16[16,2048]{1,0:T(8,128)(2,1)S(1)} %get-tuple-element.85), channel_id=1, source_target_pairs={{0,4},{1,5},{2,6},{3,7},{4,0},{5,1},{6,2},{7,3},{8,12},{9,13},{10,... | collective-permute-start | bytes 196616 | tf_op jit(solution)/shard_map/ppermute | solution.py:615
  77.3 7.9 %collective-permute-start.11 = (bf16[16,2048]{1,0:T(8,128)(2,1)S(1)}, bf16[16,2048]{1,0:T(8,128)(2,1)S(1)}, u32[]{:S(2)}, u32[]{:S(2)}) collective-permute-start(bf16[16,2048]{1,0:T(8,128)(2,1)S(1)} %get-tuple-element.86), channel_id=1, source_target_pairs={{0,5},{1,4},{2,7},{3,6},{4,1},{5,0},{6,3},{7,2},{8,13},{9,12},{10,... | collective-permute-start | bytes 196616 | tf_op jit(solution)/shard_map/ppermute | solution.py:615
  79.6 6.0 %collective-permute-start.12 = (bf16[16,2048]{1,0:T(8,128)(2,1)S(1)}, bf16[16,2048]{1,0:T(8,128)(2,1)S(1)}, u32[]{:S(2)}, u32[]{:S(2)}) collective-permute-start(bf16[16,2048]{1,0:T(8,128)(2,1)S(1)} %get-tuple-element.87), channel_id=1, source_target_pairs={{0,6},{1,7},{2,4},{3,5},{4,2},{5,3},{6,0},{7,1},{8,14},{9,15},{10,... | collective-permute-start | bytes 196616 | tf_op jit(solution)/shard_map/ppermute | solution.py:615
  80.8 5.5 %collective-permute-start.13 = (bf16[16,2048]{1,0:T(8,128)(2,1)S(1)}, bf16[16,2048]{1,0:T(8,128)(2,1)S(1)}, u32[]{:S(2)}, u32[]{:S(2)}) collective-permute-start(bf16[16,2048]{1,0:T(8,128)(2,1)S(1)} %get-tuple-element.88), channel_id=1, source_target_pairs={{0,7},{1,6},{2,5},{3,4},{4,3},{5,2},{6,1},{7,0},{8,15},{9,14},{10,... | collective-permute-start | bytes 196616 | tf_op jit(solution)/shard_map/ppermute | solution.py:615
